TPU v7x, 32 devices: a whole 2x2x4 slice. The times are simulated.
32 devices in a mesh: dp: 8 (over y, x, core), tile: 4 (over z).
Axes of the slice: x: 2, y: 2, z: 4, core: 2. Of those that a mesh axis runs over, the one named last changes fastest.
Arguments:
- vit_tokens: bfloat16 [16, 576, 1024], P('dp', 'tile'), may hold values from -6 to 6
- hires_map: bfloat16 [16, 32, 32, 1536], P('dp', 'tile'), may hold values from -6 to 6
- norm1_gain: float32 [1024], replicated, may hold values from 0.5 to 1.5
- norm1_shift: float32 [1024], replicated, may hold values from -1.75 to 1.75
- qkv_weight: bfloat16 [1024, 3072], P('dp'), may hold values from -0.1875 to 0.1875
- attn_weight: bfloat16 [1024, 1024], P('dp'), may hold values from -0.75 to 0.75
- norm2_gain: float32 [1024], replicated, may hold values from 0.5 to 1.5
- norm2_shift: float32 [1024], replicated, may hold values from -1.75 to 1.75
- vit_fc1: bfloat16 [1024, 4096], P('dp'), may hold values from -0.1875 to 0.1875
- vit_fc2: bfloat16 [4096, 1024], P('dp'), may hold values from -0.09375 to 0.09375
- conv_kernel: float32 [49, 1536], replicated, may hold values from -0.875 to 0.875
- conv_gain: float32 [1536], replicated, may hold values from 0.5 to 1.5
- conv_shift: float32 [1536], replicated, may hold values from -1.75 to 1.75
- conv_fc1: bfloat16 [1536, 6144], P('dp'), may hold values from -0.15625 to 0.15625
- conv_fc2: bfloat16 [6144, 1536], P('dp'), may hold values from -0.078125 to 0.078125
- layer_scale: float32 [1536], replicated, may hold values from 0.5 to 1.5
- adapter_weight: bfloat16 [1536, 1024], P('dp'), may hold values from -0.15625 to 0.15625
- adapter_bias: float32 [1024], replicated, may hold values from -1.75 to 1.75
- adapter_kernel: float32 [9, 1024], replicated, may hold values from -3.5 to 3.5
- adapter_gate: float32 [1024], replicated, may hold values from 0.4 to 1.2
- proj_fc1: bfloat16 [1024, 4096], P('dp'), may hold values from -0.1875 to 0.1875
- proj_bias1: float32 [4096], replicated, may hold values from -1.75 to 1.75
- proj_fc2: bfloat16 [4096, 4096], P('dp'), may hold values from -0.09375 to 0.09375
- proj_bias2: float32 [4096], replicated, may hold values from -1.75 to 1.75
- projected_cot: bfloat16 [16, 576, 4096], P('dp', 'tile'), may hold values from -6 to 6
- hires_cot: bfloat16 [16, 32, 32, 1536], P('dp', 'tile'), may hold values from -6 to 6
Outputs:
- projected: bfloat16 [16, 576, 4096], P('dp', 'tile')
- hires_out: bfloat16 [16, 32, 32, 1536], P('dp', 'tile')
- tokens_grad: float32 [16, 576, 1024], P('dp', 'tile')
- hires_grad: float32 [16, 32, 32, 1536], P('dp', 'tile')
- adapter_weight_grad: float32 [1536, 1024], P(('dp', 'tile'))
- adapter_bias_grad: float32 [1024], replicated
- adapter_kernel_grad: float32 [9, 1024], replicated
- adapter_gate_grad: float32 [1024], replicated
- proj_fc1_grad: float32 [1024, 4096], P(('dp', 'tile'))
- proj_bias1_grad: float32 [4096], replicated
- proj_fc2_grad: float32 [4096, 4096], P(('dp', 'tile'))
- proj_bias2_grad: float32 [4096], replicated
All inputs are finite; a program needn't handle non-finite values.
Results may differ from a plain program's by a relative error of at most 0.014.
Values may be sent and summed in bfloat16 or wider, within the bound.
A program may use at most 384 MiB of HBM per device.

v0:
```python
import jax
import jax.numpy as jnp
from jax import lax
from jax.sharding import PartitionSpec as P

HEADS = 16
GV = 24


EPS_VIT = 1e-05
EPS_CONV = 1e-06
HIGHEST_PRECISION = lax.Precision.HIGHEST


def padded(shard, sides, width):
    for axis, dim in sides:
        size, length = (lax.axis_size(axis), shard.shape[dim])
        up = [(i, (i + 1) % size) for i in range(size - 1)]
        down = [(j, i) for i, j in up]
        last = lax.slice_in_dim(shard, length - width, length, axis=dim)
        leading = lax.slice_in_dim(shard, 0, width, axis=dim)
        before = lax.ppermute(last, axis, up)
        after = lax.ppermute(leading, axis, down)
        shard = jnp.concatenate([before, shard, after], axis=dim)
    return shard


def layer_norm(values, norm_gain, norm_shift, epsilon):
    average = jnp.mean(values, axis=-1, keepdims=True)
    centred = values - average
    spread = jnp.mean(centred * centred, axis=-1, keepdims=True)
    return centred * lax.rsqrt(spread + epsilon) * norm_gain + norm_shift


def product(left, right):
    return jnp.dot(left, right, preferred_element_type=jnp.float32)


def times_transposed(left, right):
    return lax.dot_general(
        left, right, (((1,), (1,)), ((), ())), preferred_element_type=jnp.float32
    )


def row_contract(left, right):
    return lax.dot_general(
        left, right, (((0,), (0,)), ((), ())), preferred_element_type=jnp.float32
    )


def pool_matrix(count_out, count_in):
    out_index = jnp.arange(count_out)[:, None]
    in_index = jnp.arange(count_in)[None, :]
    first_row = out_index * count_in // count_out
    end_row = ((out_index + 1) * count_in + count_out - 1) // count_out
    member = (in_index >= first_row) & (in_index < end_row)
    return member.astype(jnp.float32) / (end_row - first_row).astype(jnp.float32)


def depthwise_rows(framed_rows, kernel, reach):
    width = 2 * reach + 1
    row_count = framed_rows.shape[1] - 2 * reach
    col_count = framed_rows.shape[2]
    framed = jnp.pad(framed_rows, ((0, 0), (0, 0), (reach, reach), (0, 0)))
    total = jnp.zeros(
        (framed_rows.shape[0], row_count, col_count, framed_rows.shape[3]), jnp.float32
    )
    for row_off in range(width):
        for col_off in range(width):
            window = framed[:, row_off : row_off + row_count, col_off : col_off + col_count]
            total = total + window * kernel[row_off * width + col_off]
    return total


def kernel_terms(framed_rows, grad_map, reach):
    width = 2 * reach + 1
    row_count = grad_map.shape[1]
    col_count = grad_map.shape[2]
    framed = jnp.pad(framed_rows, ((0, 0), (0, 0), (reach, reach), (0, 0)))
    kernel_rows = []
    for row_off in range(width):
        for col_off in range(width):
            window = framed[:, row_off : row_off + row_count, col_off : col_off + col_count]
            kernel_rows.append(jnp.sum(window * grad_map, axis=(0, 1, 2)))
    return jnp.stack(kernel_rows)


def summed_rows(term_fn, total_rows):
    result = lax.psum_scatter(
        term_fn(
            jnp.int32(0),
            lax.axis_size(("dp", "tile"))
            * (total_rows // (lax.axis_size("dp") * lax.axis_size("tile"))),
        ),
        ("dp", "tile"),
        scatter_dimension=0,
        tiled=True,
    )
    return result


def body(
    vit_tokens,
    hires_map,
    norm1_gain,
    norm1_shift,
    qkv_weight,
    attn_weight,
    norm2_gain,
    norm2_shift,
    vit_fc1,
    vit_fc2,
    conv_kernel,
    conv_gain,
    conv_shift,
    conv_fc1,
    conv_fc2,
    layer_scale,
    adapter_weight,
    adapter_bias,
    adapter_kernel,
    adapter_gate,
    proj_fc1,
    proj_bias1,
    proj_fc2,
    proj_bias2,
    projected_cot,
    hires_cot,
):
    qkv_full, attn_full, vit_up, vit_down = (
        lax.all_gather(qkv_weight, "dp", axis=0, tiled=True),
        lax.all_gather(attn_weight, "dp", axis=0, tiled=True),
        lax.all_gather(vit_fc1, "dp", axis=0, tiled=True),
        lax.all_gather(vit_fc2, "dp", axis=0, tiled=True),
    )
    conv_up, conv_down = (
        lax.all_gather(conv_fc1, "dp", axis=0, tiled=True),
        lax.all_gather(conv_fc2, "dp", axis=0, tiled=True),
    )
    adapter_full, proj_up, proj_down = (
        lax.all_gather(adapter_weight, "dp", axis=0, tiled=True),
        lax.all_gather(proj_fc1, "dp", axis=0, tiled=True),
        lax.all_gather(proj_fc2, "dp", axis=0, tiled=True),
    )
    images = vit_tokens.shape[0]
    tok_rows = vit_tokens.shape[1]
    model_width = vit_tokens.shape[2]
    head_size = model_width // HEADS
    scale = head_size ** (-0.5)
    vit_rows = tok_rows // GV
    hires_rows = hires_map.shape[1]
    hires_cols = hires_map.shape[2]
    channels = hires_map.shape[3]
    tokens_float = vit_tokens.astype(jnp.float32)
    normed_a, norm_a_back = jax.vjp(
        lambda values: layer_norm(values, norm1_gain, norm1_shift, EPS_VIT), tokens_float
    )
    qkv_all = product(normed_a.astype(jnp.bfloat16).reshape(-1, model_width), qkv_full).astype(
        jnp.bfloat16
    )
    qkv_all = qkv_all.reshape(images, tok_rows, 3 * model_width)
    query = qkv_all[..., :model_width].reshape(images, tok_rows, HEADS, head_size)
    key_value = lax.all_gather(qkv_all[..., model_width:], "tile", axis=1, tiled=True)
    seq_tokens = key_value.shape[1]
    keys_all = key_value[..., :model_width].reshape(images, seq_tokens, HEADS, head_size)
    values_all = key_value[..., model_width:].reshape(images, seq_tokens, HEADS, head_size)
    scores = (
        jnp.einsum("ithe,ishe->ihts", query, keys_all, preferred_element_type=jnp.float32) * scale
    )
    probs = jax.nn.softmax(scores, axis=-1)
    probs_low = probs.astype(jnp.bfloat16)
    attended = jnp.einsum(
        "ihts,ishe->ithe", probs_low, values_all, preferred_element_type=jnp.float32
    )
    attended = attended.astype(jnp.bfloat16).reshape(-1, model_width)
    hidden_a = tokens_float + product(attended, attn_full).reshape(images, tok_rows, model_width)
    normed_b, norm_b_back = jax.vjp(
        lambda values: layer_norm(values, norm2_gain, norm2_shift, EPS_VIT), hidden_a
    )
    up_a = product(normed_b.astype(jnp.bfloat16).reshape(-1, model_width), vit_up)
    act_a, gelu_a_back = jax.vjp(jax.nn.gelu, up_a)
    vit_out = hidden_a + product(act_a.astype(jnp.bfloat16), vit_down).reshape(
        images, tok_rows, model_width
    )
    hires_float = hires_map.astype(jnp.float32)
    hires_framed = padded(hires_map, (("tile", 1),), 3)
    conv_in = depthwise_rows(hires_framed, conv_kernel, 3)
    normed_c, norm_c_back = jax.vjp(
        lambda values: layer_norm(values, conv_gain, conv_shift, EPS_CONV), conv_in
    )
    up_c = product(normed_c.astype(jnp.bfloat16).reshape(-1, channels), conv_up)
    act_c, gelu_c_back = jax.vjp(jax.nn.gelu, up_c)
    refined = hires_float + layer_scale * product(act_c.astype(jnp.bfloat16), conv_down).reshape(
        hires_map.shape
    )
    hires_out = refined.astype(jnp.bfloat16)
    row_pool = pool_matrix(vit_rows, hires_rows)
    col_pool = pool_matrix(GV, hires_cols)
    pooled = jnp.einsum("ar,irch->iach", row_pool, refined, precision=HIGHEST_PRECISION)
    pooled = jnp.einsum("bc,iach->iabh", col_pool, pooled, precision=HIGHEST_PRECISION)
    pooled_low = pooled.astype(jnp.bfloat16).reshape(-1, channels)
    adapted = (product(pooled_low, adapter_full) + adapter_bias).astype(jnp.bfloat16)
    adapted = adapted.reshape(images, vit_rows, GV, model_width)
    adapted_framed = padded(adapted, (("tile", 1),), 1)
    mixed_map = depthwise_rows(adapted_framed, adapter_kernel, 1).reshape(
        images, tok_rows, model_width
    )
    gate_value = jnp.tanh(adapter_gate)
    merged = vit_out + gate_value * mixed_map
    merged_low = merged.astype(jnp.bfloat16).reshape(-1, model_width)
    pre_act = product(merged_low, proj_up) + proj_bias1
    act_p, gelu_p_back = jax.vjp(jax.nn.gelu, pre_act)
    act_p_low = act_p.astype(jnp.bfloat16)
    projected = (
        (product(act_p_low, proj_down) + proj_bias2)
        .astype(jnp.bfloat16)
        .reshape(images, tok_rows, -1)
    )
    out_grad = projected_cot.reshape(-1, projected_cot.shape[2])
    bias2_grad = jnp.sum(out_grad.astype(jnp.float32), axis=0)
    fc2_grad = summed_rows(
        lambda first_row, row_count: row_contract(act_p_low, out_grad), proj_down.shape[0]
    )
    pre_grad = gelu_p_back(times_transposed(out_grad, proj_down))[0].astype(jnp.bfloat16)
    bias1_grad = jnp.sum(pre_grad.astype(jnp.float32), axis=0)
    fc1_grad = summed_rows(
        lambda first_row, row_count: row_contract(merged_low, pre_grad), model_width
    )
    merged_grad = times_transposed(pre_grad, proj_up).reshape(images, tok_rows, model_width)
    gate_grad = jnp.sum(merged_grad * mixed_map, axis=(0, 1)) * (1.0 - gate_value * gate_value)
    mixed_grad = (gate_value * merged_grad).reshape(images, vit_rows, GV, model_width)
    mixed_framed = padded(mixed_grad.astype(jnp.bfloat16), (("tile", 1),), 1).astype(
        mixed_grad.dtype
    )
    kernel_grad = kernel_terms(adapted_framed, mixed_grad, 1)
    adapted_grad = (
        depthwise_rows(mixed_framed, adapter_kernel[::-1], 1)
        .astype(jnp.bfloat16)
        .reshape(-1, model_width)
    )
    bias_a_grad = jnp.sum(adapted_grad.astype(jnp.float32), axis=0)
    adapter_grad = summed_rows(
        lambda first_row, row_count: row_contract(pooled_low, adapted_grad), channels
    )
    pooled_grad = times_transposed(adapted_grad, adapter_full).reshape(
        images, vit_rows, GV, channels
    )
    unpooled = jnp.einsum("bc,iabh->iach", col_pool, pooled_grad, precision=HIGHEST_PRECISION)
    unpooled = jnp.einsum("ar,iach->irch", row_pool, unpooled, precision=HIGHEST_PRECISION)
    refined_grad = hires_cot.astype(jnp.float32) + unpooled
    branch_grad = (layer_scale * refined_grad).astype(jnp.bfloat16).reshape(-1, channels)
    up_c_grad = gelu_c_back(times_transposed(branch_grad, conv_down))[0].astype(jnp.bfloat16)
    conv_in_grad = norm_c_back(times_transposed(up_c_grad, conv_up).reshape(hires_map.shape))[0]
    conv_framed = padded(conv_in_grad.astype(jnp.bfloat16), (("tile", 1),), 3).astype(
        conv_in_grad.dtype
    )
    hires_grad = refined_grad + depthwise_rows(conv_framed, conv_kernel[::-1], 3)
    down_grad = merged_grad.astype(jnp.bfloat16).reshape(-1, model_width)
    up_a_grad = gelu_a_back(times_transposed(down_grad, vit_down))[0].astype(jnp.bfloat16)
    hidden_grad = (
        merged_grad
        + norm_b_back(times_transposed(up_a_grad, vit_up).reshape(images, tok_rows, model_width))[0]
    )
    attn_grad = hidden_grad.astype(jnp.bfloat16).reshape(-1, model_width)
    attended_grad = (
        times_transposed(attn_grad, attn_full)
        .astype(jnp.bfloat16)
        .reshape(images, tok_rows, HEADS, head_size)
    )
    probs_grad = jnp.einsum(
        "ithe,ishe->ihts", attended_grad, values_all, preferred_element_type=jnp.float32
    )
    scores_grad = (
        probs * (probs_grad - jnp.sum(probs * probs_grad, axis=-1, keepdims=True))
    ).astype(jnp.bfloat16)
    query_grad = (
        jnp.einsum("ihts,ishe->ithe", scores_grad, keys_all, preferred_element_type=jnp.float32)
        * scale
    )
    keys_grad = (
        jnp.einsum("ihts,ithe->ishe", scores_grad, query, preferred_element_type=jnp.float32)
        * scale
    )
    values_grad = jnp.einsum(
        "ihts,ithe->ishe", probs_low, attended_grad, preferred_element_type=jnp.float32
    )
    pair_grad = jnp.concatenate(
        [
            keys_grad.reshape(images, seq_tokens, model_width),
            values_grad.reshape(images, seq_tokens, model_width),
        ],
        axis=-1,
    )
    pair_local = lax.psum_scatter(
        pair_grad.astype(jnp.bfloat16), "tile", scatter_dimension=1, tiled=True
    ).astype(jnp.float32)
    qkv_grad = jnp.concatenate(
        [query_grad.reshape(images, tok_rows, model_width), pair_local], axis=-1
    )
    qkv_grad = qkv_grad.astype(jnp.bfloat16).reshape(-1, 3 * model_width)
    tokens_grad = (
        hidden_grad
        + norm_a_back(times_transposed(qkv_grad, qkv_full).reshape(images, tok_rows, model_width))[
            0
        ]
    )
    bias2_grad, bias1_grad, bias_a_grad, kernel_grad, gate_grad = lax.psum(
        (bias2_grad, bias1_grad, bias_a_grad, kernel_grad, gate_grad), ("dp", "tile")
    )
    return (
        projected,
        hires_out,
        tokens_grad,
        hires_grad,
        adapter_grad,
        bias_a_grad,
        kernel_grad,
        gate_grad,
        fc1_grad,
        bias1_grad,
        fc2_grad,
        bias2_grad,
    )


def solution(mesh):
    in_specs = (
        P("dp", "tile", None),
        P("dp", "tile", None, None),
        P(),
        P(),
        P("dp", None),
        P("dp", None),
        P(),
        P(),
        P("dp", None),
        P("dp", None),
        P(),
        P(),
        P(),
        P("dp", None),
        P("dp", None),
        P(),
        P("dp", None),
        P(),
        P(),
        P(),
        P("dp", None),
        P(),
        P("dp", None),
        P(),
        P("dp", "tile", None),
        P("dp", "tile", None, None),
    )
    out_specs = (
        P("dp", "tile", None),
        P("dp", "tile", None, None),
        P("dp", "tile", None),
        P("dp", "tile", None, None),
        P(("dp", "tile"), None),
        P(),
        P(),
        P(),
        P(("dp", "tile"), None),
        P(),
        P(("dp", "tile"), None),
        P(),
    )
    return jax.shard_map(body, mesh=mesh, in_specs=in_specs, out_specs=out_specs, check_vma=False)
```

profile of v0, /device:TPU:0, one launch (start us, length us, event | category | flops | bytes accessed | tf_op | source)
XLA Modules:
  0.0 2972.8 jit_solution(7688494781821037049)
XLA Ops:
  13.1 45.0 %all-gather.11.cloned.1.call-done = bf16[1024,3072]{1,0:T(8,128)(2,1)} async-done(((bf16[128,3072]{1,0:T(8,128)(2,1)}), bf16[1024,3072]{1,0:T(8,128)(2,1)}) %all-gather.11.cloned.1.call-update) | async-done | bytes 6291472 | tf_op jit(solution)/shard_map/all_gather | solution.py:131
  88.8 13.1 collective-permute-done
  113.7 29.2 fusion.306
  149.9 15.1 all-gather.13.cloned.1.call-done
  179.2 9.8 fusion.314
  189.0 8.9 fusion.191
  201.4 50.3 %all-gather.17.cloned.1.call-done = bf16[1024,4096]{1,0:T(8,128)(2,1)} async-done(((bf16[128,4096]{1,0:T(8,128)(2,1)}), bf16[1024,4096]{1,0:T(8,128)(2,1)}) %all-gather.17.cloned.1.call-update) | async-done | bytes 8388624 | tf_op jit(solution)/shard_map/all_gather | solution.py:133
  251.6 7.6 fusion.316
  259.2 92.9 %all-gather.21.cloned.1.call-done = bf16[1536,6144]{1,0:T(8,128)(2,1)} async-done(((bf16[192,6144]{1,0:T(8,128)(2,1)}), bf16[1536,6144]{1,0:T(8,128)(2,1)}) %all-gather.21.cloned.1.call-update) | async-done | bytes 18874384 | tf_op jit(solution)/shard_map/all_gather | solution.py:137
  352.1 17.0 fusion.317
  369.1 83.5 %all-gather.23.cloned.1.call-done = bf16[6144,1536]{1,0:T(8,128)(2,1)} async-done(((bf16[768,1536]{1,0:T(8,128)(2,1)}), bf16[6144,1536]{1,0:T(8,128)(2,1)}) %all-gather.23.cloned.1.call-update) | async-done | bytes 18874384 | tf_op jit(solution)/shard_map/all_gather | solution.py:138
  452.6 19.1 fusion.12
  496.3 46.9 %all-gather.19.cloned.1.call-done = bf16[4096,1024]{1,0:T(8,128)(2,1)} async-done(((bf16[512,1024]{1,0:T(8,128)(2,1)}), bf16[4096,1024]{1,0:T(8,128)(2,1)}) %all-gather.19.cloned.1.call-update) | async-done | bytes 8388624 | tf_op jit(solution)/shard_map/all_gather | solution.py:134
  543.2 7.8 fusion.166
  553.9 152.0 %all-gather.29.cloned.1.call-done = bf16[4096,4096]{1,0:T(8,128)(2,1)} async-done(((bf16[512,4096]{1,0:T(8,128)(2,1)}), bf16[4096,4096]{1,0:T(8,128)(2,1)}) %all-gather.29.cloned.1.call-update) | async-done | bytes 33554448 | tf_op jit(solution)/shard_map/all_gather | solution.py:143
  705.9 19.1 fusion.318
  725.0 37.1 %all-gather.27.cloned.1.call-done = bf16[1024,4096]{1,0:T(8,128)(2,1)} async-done(((bf16[128,4096]{1,0:T(8,128)(2,1)}), bf16[1024,4096]{1,0:T(8,128)(2,1)}) %all-gather.27.cloned.1.call-update) | async-done | bytes 8388624 | tf_op jit(solution)/shard_map/all_gather | solution.py:142
  762.1 12.4 convert_reduce_fusion.1
  777.9 12.5 fusion.172
  799.5 7.4 fusion.177
  806.9 8.5 multiply_reduce_fusion
  819.7 8.8 multiply_convert_fusion.1
  867.7 8.1 fusion.320
  877.5 28.9 fusion.302
  912.2 8.6 multiply_convert_fusion.6
  922.5 30.2 %fusion.19 = f32[512,1536]{1,0:T(8,128)} fusion(bf16[1536,6144]{1,0:T(8,128)(2,1)} %all-gather.21.cloned.1.call-done, f32[512,6144]{1,0:T(8,128)} %fusion.317, bf16[512,1536]{1,0:T(8,128)(2,1)} %bitcast.195, bf16[6144,1536]{1,0:T(8,128)(2,1)} %all-gather.23.cloned.1.call-done), kind=kOutput, calls=%fused_computation.72 | convolution fusion | flops 19390267392 | bytes 55050240 | tf_op jit(solution)/shard_map/dot_general | solution.py:40
  970.4 19.3 fusion.22
  1005.0 25.1 fusion.154
  1043.1 16.7 all-reduce.7.cloned.1.call-done
  1059.8 121.6 %reduce-scatter.7.cloned.1.call-done = f32[48,1024]{1,0:T(8,128)} async-done(((f32[1536,1024]{1,0:T(8,128)}), f32[48,1024]{1,0:T(8,128)}) %reduce-scatter.7.cloned.1.call-update) | async-done | bytes 196624 | tf_op jit(solution)/shard_map/reduce_scatter | solution.py:89
  1181.4 366.3 %reduce-scatter.9.cloned.1.call-done = f32[32,4096]{1,0:T(8,128)} async-done(((f32[1024,4096]{1,0:T(8,128)}), f32[32,4096]{1,0:T(8,128)}) %reduce-scatter.9.cloned.1.call-update) | async-done | bytes 524304 | tf_op jit(solution)/shard_map/reduce_scatter | solution.py:89
  1547.8 1411.5 %reduce-scatter.11.cloned.1.call-done = f32[128,4096]{1,0:T(8,128)} async-done(((f32[4096,4096]{1,0:T(8,128)}), f32[128,4096]{1,0:T(8,128)}) %reduce-scatter.11.cloned.1.call-update) | async-done | bytes 2097168 | tf_op jit(solution)/shard_map/reduce_scatter | solution.py:89
  (499 shorter events, 215.4 us)
Async XLA Ops:
  7.2 51.0 %all-gather.11.cloned.1.call-start = ((), (), s32[]{:S(2)}) async-start(), calls=%async_computation.4 | async-start | bytes 7077888 | tf_op jit(solution)/shard_map/all_gather | solution.py:131
  7.9 157.1 %all-gather.13.cloned.1.call-start = ((), (), s32[]{:S(2)}) async-start(), calls=%async_computation.5 | async-start | bytes 5898240 | tf_op jit(solution)/shard_map/all_gather | solution.py:163
  65.3 132.6 %all-gather.15.cloned.1.call-start = ((), (), s32[]{:S(2)}) async-start(), calls=%async_computation.6 | async-start | bytes 2359296 | tf_op jit(solution)/shard_map/all_gather | solution.py:132
  66.0 185.6 %all-gather.17.cloned.1.call-start = ((), (), s32[]{:S(2)}) async-start(), calls=%async_computation.7 | async-start | bytes 9437184 | tf_op jit(solution)/shard_map/all_gather | solution.py:133
  66.6 285.5 %all-gather.21.cloned.1.call-start = ((), (), s32[]{:S(2)}) async-start(), calls=%async_computation.9 | async-start | bytes 21233664 | tf_op jit(solution)/shard_map/all_gather | solution.py:137
  67.2 385.5 %all-gather.23.cloned.1.call-start = ((), (), s32[]{:S(2)}) async-start(), calls=%async_computation.10 | async-start | bytes 21233664 | tf_op jit(solution)/shard_map/all_gather | solution.py:138
  67.8 419.1 %all-gather.25.cloned.1.call-start = ((), (), s32[]{:S(2)}) async-start(), calls=%async_computation.11 | async-start | bytes 3538944 | tf_op jit(solution)/shard_map/all_gather | solution.py:141
  68.5 474.7 %all-gather.19.cloned.1.call-start = ((), (), s32[]{:S(2)}) async-start(), calls=%async_computation.8 | async-start | bytes 9437184 | tf_op jit(solution)/shard_map/all_gather | solution.py:134
  69.3 636.6 %all-gather.29.cloned.1.call-start = ((), (), s32[]{:S(2)}) async-start(), calls=%async_computation.13 | async-start | bytes 37748736 | tf_op jit(solution)/shard_map/all_gather | solution.py:143
  70.0 692.0 %all-gather.27.cloned.1.call-start = ((), (), s32[]{:S(2)}) async-start(), calls=%async_computation.12 | async-start | bytes 9437184 | tf_op jit(solution)/shard_map/all_gather | solution.py:142
  70.2 39.7 %collective-permute-start.1 = (bf16[2,3,32,1536]{3,2,1,0:T(8,128)(2,1)S(1)}, bf16[2,3,32,1536]{3,2,1,0:T(8,128)(2,1)S(1)}, u32[]{:S(2)}, u32[]{:S(2)}) collective-permute-start(bf16[2,3,32,1536]{3,2,1,0:T(8,128)(2,1)S(1)} %get-tuple-element.129), channel_id=1, source_target_pairs={{1,0},{2,1},{3,2},{5,4},{6,5},{7,6},{9,8},{10,9},{11,10},{13,12},{... | collective-permute-start | bytes 1769480 | tf_op jit(solution)/shard_map/ppermute | solution.py:23
  71.5 30.5 %collective-permute-start = (bf16[2,3,32,1536]{3,2,1,0:T(8,128)(2,1)S(1)}, bf16[2,3,32,1536]{3,2,1,0:T(8,128)(2,1)}, u32[]{:S(2)}, u32[]{:S(2)}) collective-permute-start(bf16[2,3,32,1536]{3,2,1,0:T(8,128)(2,1)S(1)} %get-tuple-element.128), channel_id=1, source_target_pairs={{0,1},{1,2},{2,3},{4,5},{5,6},{6,7},{8,9},{9,10},{10,11},{12,13},{... | collective-permute-start | bytes 1769480 | tf_op jit(solution)/shard_map/ppermute | solution.py:22
  76.9 958.6 %reduce-scatter.5.cloned.1.call-start = ((), (), s32[]{:S(2)}) async-start(), calls=%async_computation.14 | async-start | bytes 5898240 | tf_op jit(solution)/shard_map/reduce_scatter | solution.py:294
  369.1 102.7 %copy-start.44 = (f32[1536]{0:T(1024)S(1)}, f32[1536]{0:T(1024)}, u32[]{:S(2)}) copy-start(f32[1536]{0:T(1024)} %param.41) | copy-start | bytes 18436
  369.1 102.7 %copy-start.160 = (f32[6]{0:T(128)S(1)}, f32[6]{0:T(128)}, u32[]{:S(2)}) copy-start(f32[6]{0:T(128)} %subtract_convert_fusion.1) | copy-start | bytes 76
  369.1 102.7 %copy-start.162 = (s32[6]{0:T(128)S(1)}, s32[6]{0:T(128)}, u32[]{:S(2)}) copy-start(s32[6]{0:T(128)} %get-tuple-element.159) | copy-start | bytes 76
  369.1 102.7 %copy-start.164 = (s32[6]{0:T(128)S(1)}, s32[6]{0:T(128)}, u32[]{:S(2)}) copy-start(s32[6]{0:T(128)} %get-tuple-element.160) | copy-start | bytes 76
  489.9 61.6 %copy-start.19 = (bf16[288,1024]{1,0:T(8,128)(2,1)}, bf16[288,1024]{1,0:T(8,128)(2,1)S(1)}, u32[]{:S(2)}) copy-start(bf16[288,1024]{1,0:T(8,128)(2,1)S(1)} %fusion.201) | copy-start | bytes 1769476
  489.9 61.2 %collective-permute-start.3 = (bf16[2,1,24,1024]{3,2,1,0:T(8,128)(2,1)S(1)}, bf16[2,1,24,1024]{3,2,1,0:T(8,128)(2,1)S(1)}, u32[]{:S(2)}, u32[]{:S(2)}) collective-permute-start(bf16[2,1,24,1024]{3,2,1,0:T(8,128)(2,1)S(1)} %get-tuple-element.134), channel_id=1, source_target_pairs={{1,0},{2,1},{3,2},{5,4},{6,5},{7,6},{9,8},{10,9},{11,10},{13,12},{... | collective-permute-start | bytes 294920 | tf_op jit(solution)/shard_map/ppermute | solution.py:23
  491.2 60.3 %copy-start.132 = (f32[1,1024]{1,0:T(1,128)S(1)}, f32[1,1024]{1,0:T(1,128)}, u32[]{:S(2)}) copy-start(f32[1,1024]{1,0:T(1,128)} %get-tuple-element.137) | copy-start | bytes 12292
  491.2 60.3 %copy-start.133 = (f32[1,1024]{1,0:T(1,128)S(1)}, f32[1,1024]{1,0:T(1,128)}, u32[]{:S(2)}) copy-start(f32[1,1024]{1,0:T(1,128)} %get-tuple-element.138) | copy-start | bytes 12292
  491.3 59.8 %collective-permute-start.2 = (bf16[2,1,24,1024]{3,2,1,0:T(8,128)(2,1)S(1)}, bf16[2,1,24,1024]{3,2,1,0:T(8,128)(2,1)S(1)}, u32[]{:S(2)}, u32[]{:S(2)}) collective-permute-start(bf16[2,1,24,1024]{3,2,1,0:T(8,128)(2,1)S(1)} %get-tuple-element.133), channel_id=1, source_target_pairs={{0,1},{1,2},{2,3},{4,5},{5,6},{6,7},{8,9},{9,10},{10,11},{12,13},{... | collective-permute-start | bytes 294920 | tf_op jit(solution)/shard_map/ppermute | solution.py:22
  553.9 208.1 %copy-start.27 = (bf16[2,144,1024]{2,1,0:T(8,128)(2,1)}, bf16[2,144,1024]{2,1,0:T(8,128)(2,1)S(1)}, u32[]{:S(2)}) copy-start(bf16[2,144,1024]{2,1,0:T(8,128)(2,1)S(1)} %fusion.243) | copy-start | bytes 1769476
  777.9 66.3 %copy-start.14 = (f32[288,1024]{1,0:T(8,128)}, f32[288,1024]{1,0:T(8,128)S(1)}, u32[]{:S(2)}) copy-start(f32[288,1024]{1,0:T(8,128)S(1)} %get-tuple-element.158) | copy-start | bytes 3538948
  841.5 218.4 %all-reduce.7.cloned.1.call-start = ((), (), s32[]{:S(2)}) async-start(), calls=%async_computation.18 | async-start | bytes 212992 | tf_op jit(solution)/shard_map/psum | solution.py:307
  846.8 12.1 collective-permute-start.5
  848.1 10.8 collective-permute-start.4
  861.4 320.0 %reduce-scatter.7.cloned.1.call-start = ((), (), s32[]{:S(2)}) async-start(), calls=%async_computation.15 | async-start | bytes 6488064 | tf_op jit(solution)/shard_map/reduce_scatter | solution.py:89
  865.9 681.9 %reduce-scatter.9.cloned.1.call-start = ((), (), s32[]{:S(2)}) async-start(), calls=%async_computation.16 | async-start | bytes 17301504 | tf_op jit(solution)/shard_map/reduce_scatter | solution.py:89
  875.9 2083.4 %reduce-scatter.11.cloned.1.call-start = ((), (), s32[]{:S(2)}) async-start(), calls=%async_computation.17 | async-start | bytes 69206016 | tf_op jit(solution)/shard_map/reduce_scatter | solution.py:89
  962.5 37.0 %collective-permute-start.7 = (bf16[2,3,32,1536]{3,2,1,0:T(8,128)(2,1)}, bf16[2,3,32,1536]{3,2,1,0:T(8,128)(2,1)}, u32[]{:S(2)}, u32[]{:S(2)}) collective-permute-start(bf16[2,3,32,1536]{3,2,1,0:T(8,128)(2,1)} %copy.105), channel_id=1, source_target_pairs={{1,0},{2,1},{3,2},{5,4},{6,5},{7,6},{9,8},{10,9},{11,10},{13,12},{... | collective-permute-start | bytes 1769480 | tf_op jit(solution)/shard_map/ppermute | solution.py:23
  964.8 36.3 %collective-permute-start.6 = (bf16[2,3,32,1536]{3,2,1,0:T(8,128)(2,1)}, bf16[2,3,32,1536]{3,2,1,0:T(8,128)(2,1)}, u32[]{:S(2)}, u32[]{:S(2)}) collective-permute-start(bf16[2,3,32,1536]{3,2,1,0:T(8,128)(2,1)} %copy.104), channel_id=1, source_target_pairs={{0,1},{1,2},{2,3},{4,5},{5,6},{6,7},{8,9},{9,10},{10,11},{12,13},{... | collective-permute-start | bytes 1769480 | tf_op jit(solution)/shard_map/ppermute | solution.py:22
  (170 other events, 1396.8 us)
Sparse Core Ops, SparseCore 0:
  9.9 48.2 all-gather.10
  65.4 99.5 all-gather.12
  166.9 28.5 all-gather.14
  197.2 54.3 all-gather.16
  253.4 98.7 all-gather.20
  353.9 98.7 all-gather.22
  454.5 32.3 all-gather.24
  488.8 54.3 all-gather.18
  545.1 160.7 all-gather.28
  707.6 54.3 all-gather.26
  841.6 87.3 reduce-scatter.4
  936.3 123.4 all-reduce.6
  1066.0 115.3 reduce-scatter.6
  1184.3 363.4 reduce-scatter.8
  1550.7 1408.5 reduce-scatter.10
where the time goes:
time: 2980 us; the launch traced here: 2970 us
  waiting for transfers between devices  2470 us (83%)
  matrix products  273 us (9%)
  other arithmetic  104 us (3%)
  local copies, waits for them, and re-layouts  78.1 us (3%)
    reduce_scatter x3, waiting for transfers between devices, summed_rows(): lax.psum_scatter(term_fn(jnp.int32(0), lax.axis_size(('dp', 'tile')) * (t...  1900 us
    all_gather x1, waiting for transfers between devices, body(): lax.all_gather(proj_fc2, 'dp', axis=0, tiled=True)  152 us
    dot_general x9, matrix products, product(): return jnp.dot(left, right, preferred_element_type=jnp.float32)  93.9 us
    all_gather x1, waiting for transfers between devices, body(): lax.all_gather(conv_fc1, 'dp', axis=0, tiled=True)  92.9 us
    all_gather x1, waiting for transfers between devices, body(): lax.all_gather(conv_fc2, 'dp', axis=0, tiled=True)  83.5 us
    dot_general x7, matrix products, times_transposed(): lax.dot_general(left, right, (((1,), (1,)), ((), ())), preferred_element_...  75.4 us
  transfers between devices with their start and end apart: 23, of which 16 were waited for; matrix products, arithmetic and copies ran while one was open for 12% of the time, Pallas kernels for 0%

commit v1 on v0

v1 whole, which is shorter than its diff:
```python
import functools

import jax
import jax.numpy as jnp
from jax import lax
from jax.experimental import pallas as pl
from jax.experimental.pallas import tpu as pltpu
from jax.sharding import PartitionSpec as P

HEADS = 16
GV = 24


EPS_VIT = 1e-05
EPS_CONV = 1e-06


def padded(shard, sides, width):
    for axis, dim in sides:
        size, length = (lax.axis_size(axis), shard.shape[dim])
        up = [(i, (i + 1) % size) for i in range(size - 1)]
        down = [(j, i) for i, j in up]
        last = lax.slice_in_dim(shard, length - width, length, axis=dim)
        leading = lax.slice_in_dim(shard, 0, width, axis=dim)
        before = lax.ppermute(last, axis, up)
        after = lax.ppermute(leading, axis, down)
        shard = jnp.concatenate([before, shard, after], axis=dim)
    return shard


def layer_norm(values, norm_gain, norm_shift, epsilon):
    average = jnp.mean(values, axis=-1, keepdims=True)
    centred = values - average
    spread = jnp.mean(centred * centred, axis=-1, keepdims=True)
    return centred * lax.rsqrt(spread + epsilon) * norm_gain + norm_shift


def product(left, right):
    return jnp.dot(left, right, preferred_element_type=jnp.float32)


def times_transposed(left, right):
    return lax.dot_general(
        left, right, (((1,), (1,)), ((), ())), preferred_element_type=jnp.float32
    )


def row_contract(left, right):
    return lax.dot_general(
        left, right, (((0,), (0,)), ((), ())), preferred_element_type=jnp.float32
    )


def pool_matrix(count_out, count_in):
    out_index = jnp.arange(count_out)[:, None]
    in_index = jnp.arange(count_in)[None, :]
    first_row = out_index * count_in // count_out
    end_row = ((out_index + 1) * count_in + count_out - 1) // count_out
    member = (in_index >= first_row) & (in_index < end_row)
    return member.astype(jnp.float32) / (end_row - first_row).astype(jnp.float32)


def with_partner(values):
    return jnp.concatenate([values, exchange(values, "tile", 1)])


def depthwise_rows(framed_rows, kernel, reach):
    width = 2 * reach + 1
    row_count = framed_rows.shape[1] - 2 * reach
    col_count = framed_rows.shape[2]
    framed = jnp.pad(framed_rows, ((0, 0), (0, 0), (reach, reach), (0, 0)))
    total = jnp.zeros(
        (framed_rows.shape[0], row_count, col_count, framed_rows.shape[3]), jnp.float32
    )
    for row_off in range(width):
        for col_off in range(width):
            window = framed[:, row_off : row_off + row_count, col_off : col_off + col_count]
            total = total + window * kernel[row_off * width + col_off]
    return total


def kernel_terms(framed_rows, grad_map, reach):
    width = 2 * reach + 1
    row_count = grad_map.shape[1]
    col_count = grad_map.shape[2]
    framed = jnp.pad(framed_rows, ((0, 0), (0, 0), (reach, reach), (0, 0)))
    kernel_rows = []
    for row_off in range(width):
        for col_off in range(width):
            window = framed[:, row_off : row_off + row_count, col_off : col_off + col_count]
            kernel_rows.append(jnp.sum(window * grad_map, axis=(0, 1, 2)))
    return jnp.stack(kernel_rows)


GELU_C = 0.7978845608028654
GELU_A = 0.044715


def gelu_value(u):
    inner = GELU_C * (u + GELU_A * (u * u * u))
    return (0.5 * u) * (1.0 + jnp.tanh(inner))


def gelu_slope(u):
    square = u * u
    t = jnp.tanh(GELU_C * (u + GELU_A * (square * u)))
    return 0.5 * (1.0 + t) + (0.5 * GELU_C) * u * (1.0 - t * t) * (1.0 + (3.0 * GELU_A) * square)


def params(mebibytes):
    return pltpu.CompilerParams(vmem_limit_bytes=mebibytes * 1024 * 1024)


def mlp_forward_kernel(x_ref, up_w_ref, down_w_ref, own_ref, other_ref, up_ref, total):
    step = pl.program_id(0)
    width = x_ref.shape[1]
    up_w = up_w_ref[...].reshape(width, -1)
    down_w = down_w_ref[...].reshape(-1, width)
    up = jnp.dot(x_ref[...], up_w, preferred_element_type=jnp.float32)
    up_ref[...] = up.astype(jnp.bfloat16)
    act = gelu_value(up).astype(jnp.bfloat16)
    part = jnp.dot(act, down_w, preferred_element_type=jnp.float32)

    @pl.when(step == 0)
    def _():
        total[...] = part

    @pl.when(step > 0)
    def _():
        total[...] += part

    @pl.when(step == pl.num_programs(0) - 1)
    def _():
        rows = own_ref.shape[0]
        own_ref[...] = total[:rows]
        other_ref[...] = total[rows:].astype(jnp.bfloat16)


def mlp_backward_kernel(y_ref, up_ref, up_w_ref, down_w_ref, own_ref, other_ref, total):
    step = pl.program_id(0)
    width = y_ref.shape[1]
    up_w = up_w_ref[...].reshape(width, -1)
    down_w = down_w_ref[...].reshape(-1, width)
    act_grad = times_transposed(y_ref[...], down_w)
    slope = gelu_slope(up_ref[...].astype(jnp.float32))
    up_grad = (act_grad * slope).astype(jnp.bfloat16)
    part = times_transposed(up_grad, up_w)

    @pl.when(step == 0)
    def _():
        total[...] = part

    @pl.when(step > 0)
    def _():
        total[...] += part

    @pl.when(step == pl.num_programs(0) - 1)
    def _():
        rows = own_ref.shape[0]
        own_ref[...] = total[:rows]
        other_ref[...] = total[rows:].astype(jnp.bfloat16)


def mlp_specs(weights, half, block):
    devices, rows, width = weights.shape
    up_rows = width // devices
    per_set = width // block
    pieces = block // half
    return (
        pl.BlockSpec((devices, up_rows, block), lambda j: (0, j // per_set, j % per_set)),
        pl.BlockSpec((pieces, half, width), lambda j: (j, 1, 0)),
    )


def mlp_cost(rows, width, hidden):
    return pl.CostEstimate(
        flops=4 * rows * width * hidden,
        bytes_accessed=4 * width * hidden + 2 * rows * hidden + 8 * rows * width,
        transcendentals=rows * hidden,
    )


def mlp_forward(x, weights, half, block):
    rows, width = x.shape
    hidden = weights.shape[0] * half
    up_spec, down_spec = mlp_specs(weights, half, block)
    whole = lambda j: (0, 0)
    return pl.pallas_call(
        mlp_forward_kernel,
        grid=(hidden // block,),
        in_specs=[pl.BlockSpec((rows, width), whole), up_spec, down_spec],
        out_specs=[
            pl.BlockSpec((rows // 2, width), whole),
            pl.BlockSpec((rows // 2, width), whole),
            pl.BlockSpec((rows, block), lambda j: (0, j)),
        ],
        out_shape=[
            jax.ShapeDtypeStruct((rows // 2, width), jnp.float32),
            jax.ShapeDtypeStruct((rows // 2, width), jnp.bfloat16),
            jax.ShapeDtypeStruct((rows, hidden), jnp.bfloat16),
        ],
        scratch_shapes=[pltpu.VMEM((rows, width), jnp.float32)],
        compiler_params=params(56),
        cost_estimate=mlp_cost(rows, width, hidden),
        name="mlp_forward",
    )(x, weights, weights)


def mlp_backward(y, up, weights, half, block):
    rows, width = y.shape
    hidden = weights.shape[0] * half
    up_spec, down_spec = mlp_specs(weights, half, block)
    whole = lambda j: (0, 0)
    return pl.pallas_call(
        mlp_backward_kernel,
        grid=(hidden // block,),
        in_specs=[
            pl.BlockSpec((rows, width), whole),
            pl.BlockSpec((rows, block), lambda j: (0, j)),
            up_spec,
            down_spec,
        ],
        out_specs=[
            pl.BlockSpec((rows // 2, width), whole),
            pl.BlockSpec((rows // 2, width), whole),
        ],
        out_shape=[
            jax.ShapeDtypeStruct((rows // 2, width), jnp.float32),
            jax.ShapeDtypeStruct((rows // 2, width), jnp.bfloat16),
        ],
        scratch_shapes=[pltpu.VMEM((rows, width), jnp.float32)],
        compiler_params=params(56),
        cost_estimate=mlp_cost(rows, width, hidden),
        name="mlp_backward",
    )(y, up, weights, weights)


LANES = 128


def conv_chunk(framed, taps_ref, columns, reach, rows, cols):
    width = 2 * reach + 1
    totals = [None] * rows
    for col_off in range(width):
        taps = [taps_ref[pl.ds(row_off * width + col_off, 1), columns] for row_off in range(width)]
        for row in range(rows + 2 * reach):
            window = framed[row, pl.ds(8 - reach + col_off, cols), :]
            for row_off in range(width):
                target = row - row_off
                if 0 <= target < rows:
                    term = window * taps[row_off]
                    totals[target] = term if totals[target] is None else totals[target] + term
    return totals


def conv_norm_kernel(reach, map_ref, taps_ref, gain_ref, shift_ref, conv_ref, normed_ref, framed):
    rows, cols, channels = conv_ref.shape[1:]
    framed[:, :8] = jnp.zeros((framed.shape[0], 8, LANES), jnp.float32)
    framed[:, 8 + cols :] = jnp.zeros((framed.shape[0], 8, LANES), jnp.float32)

    @pl.loop(0, channels // LANES)
    def _(chunk):
        columns = pl.ds(pl.multiple_of(chunk * LANES, LANES), LANES)
        framed[:, 8 : 8 + cols] = map_ref[0, :, :, columns].astype(jnp.float32)
        totals = conv_chunk(framed, taps_ref, columns, reach, rows, cols)
        for row in range(rows):
            conv_ref[0, row, :, columns] = totals[row]

    @pl.loop(0, rows)
    def _(row):
        values = conv_ref[0, row]
        average = jnp.mean(values, axis=-1, keepdims=True)
        centred = values - average
        spread = jnp.mean(centred * centred, axis=-1, keepdims=True)
        normed = centred * lax.rsqrt(spread + EPS_CONV) * gain_ref[...] + shift_ref[...]
        normed_ref[0, row] = normed.astype(jnp.bfloat16)


def conv_add_kernel(reach, map_ref, taps_ref, base_ref, out_ref, framed):
    rows, cols, channels = out_ref.shape[1:]
    framed[:, :8] = jnp.zeros((framed.shape[0], 8, LANES), jnp.float32)
    framed[:, 8 + cols :] = jnp.zeros((framed.shape[0], 8, LANES), jnp.float32)

    @pl.loop(0, channels // LANES)
    def _(chunk):
        columns = pl.ds(pl.multiple_of(chunk * LANES, LANES), LANES)
        framed[:, 8 : 8 + cols] = map_ref[0, :, :, columns].astype(jnp.float32)
        totals = conv_chunk(framed, taps_ref, columns, reach, rows, cols)
        for row in range(rows):
            out_ref[0, row, :, columns] = totals[row] + base_ref[0, row, :, columns]


def conv_specs(framed_map, reach):
    images, framed_rows, cols, channels = framed_map.shape
    rows = framed_rows - 2 * reach
    per_image = lambda i: (i, 0, 0, 0)
    map_spec = pl.BlockSpec((1, framed_rows, cols, channels), per_image)
    out_spec = pl.BlockSpec((1, rows, cols, channels), per_image)
    taps_spec = pl.BlockSpec(((2 * reach + 1) ** 2, channels), lambda i: (0, 0))
    scratch = pltpu.VMEM((framed_rows, cols + 16, LANES), jnp.float32)
    cost = pl.CostEstimate(
        flops=2 * (2 * reach + 1) ** 2 * images * rows * cols * channels,
        bytes_accessed=10 * images * rows * cols * channels,
        transcendentals=0,
    )
    return (images, rows, cols, channels), map_spec, out_spec, taps_spec, scratch, cost


def conv_norm(framed_map, taps, gain, shift, reach):
    shape, map_spec, out_spec, taps_spec, scratch, cost = conv_specs(framed_map, reach)
    row_spec = pl.BlockSpec((1, shape[3]), lambda i: (0, 0))
    return pl.pallas_call(
        functools.partial(conv_norm_kernel, reach),
        grid=(shape[0],),
        in_specs=[map_spec, taps_spec, row_spec, row_spec],
        out_specs=[out_spec, out_spec],
        out_shape=[
            jax.ShapeDtypeStruct(shape, jnp.float32),
            jax.ShapeDtypeStruct(shape, jnp.bfloat16),
        ],
        scratch_shapes=[scratch],
        compiler_params=params(32),
        cost_estimate=cost,
        name="conv_norm",
    )(framed_map, taps, gain[None], shift[None])


def conv_add(framed_map, taps, base, reach):
    shape, map_spec, out_spec, taps_spec, scratch, cost = conv_specs(framed_map, reach)
    return pl.pallas_call(
        functools.partial(conv_add_kernel, reach),
        grid=(shape[0],),
        in_specs=[map_spec, taps_spec, out_spec],
        out_specs=out_spec,
        out_shape=jax.ShapeDtypeStruct(shape, jnp.float32),
        scratch_shapes=[scratch],
        compiler_params=params(32),
        cost_estimate=cost,
        name="conv_add",
    )(framed_map, taps, base)


def head_probs(q, k, mine, scale):
    own = jnp.where(mine, q, jnp.zeros_like(q))
    scores = times_transposed(own, k) * scale
    raised = jnp.exp(scores - jnp.max(scores, axis=-1, keepdims=True))
    return raised / jnp.sum(raised, axis=-1, keepdims=True)


def attention_kernel(head_size, q_ref, k_ref, v_ref, out_ref):
    q, k, v = q_ref[0], k_ref[0], v_ref[0]
    scale = head_size ** (-0.5)
    head_of = lax.broadcasted_iota(jnp.int32, q.shape, 1) // head_size
    result = jnp.zeros(q.shape, jnp.float32)
    for head in range(q.shape[1] // head_size):
        mine = head_of == head
        probs = head_probs(q, k, mine, scale).astype(jnp.bfloat16)
        result = jnp.where(mine, product(probs, v), result)
    out_ref[0] = result.astype(jnp.bfloat16)


def attention_grad_kernel(head_size, q_ref, k_ref, v_ref, g_ref, dq_ref, dk_ref, dv_ref):
    q, k, v, grad = q_ref[0], k_ref[0], v_ref[0], g_ref[0]
    scale = head_size ** (-0.5)
    head_of = lax.broadcasted_iota(jnp.int32, q.shape, 1) // head_size
    q_grad = k_grad = v_grad = jnp.zeros(q.shape, jnp.float32)
    for head in range(q.shape[1] // head_size):
        mine = head_of == head
        probs = head_probs(q, k, mine, scale)
        probs_grad = times_transposed(jnp.where(mine, grad, jnp.zeros_like(grad)), v)
        weighted = probs * probs_grad
        scores_grad = weighted - probs * jnp.sum(weighted, axis=-1, keepdims=True)
        scores_grad = scores_grad.astype(jnp.bfloat16)
        q_grad = jnp.where(mine, product(scores_grad, k), q_grad)
        k_grad = jnp.where(mine, row_contract(scores_grad, q), k_grad)
        v_grad = jnp.where(mine, row_contract(probs.astype(jnp.bfloat16), grad), v_grad)
    dq_ref[0] = (q_grad * scale).astype(jnp.bfloat16)
    dk_ref[0] = (k_grad * scale).astype(jnp.bfloat16)
    dv_ref[0] = v_grad.astype(jnp.bfloat16)


def attention_specs(by_head):
    images, tokens, width = by_head.shape
    pairs = width // 3 // LANES
    specs = [
        pl.BlockSpec((1, tokens, LANES), lambda i, h, kind=kind: (i, 0, kind * pairs + h))
        for kind in range(3)
    ]
    one = pl.BlockSpec((1, tokens, LANES), lambda i, h: (i, 0, h))
    out = jax.ShapeDtypeStruct((images, tokens, width // 3), jnp.bfloat16)
    return (images, pairs), specs, one, out


def attention(by_head, head_size):
    grid, specs, one, out = attention_specs(by_head)
    images, tokens, width = by_head.shape
    return pl.pallas_call(
        functools.partial(attention_kernel, head_size),
        grid=grid,
        in_specs=specs,
        out_specs=one,
        out_shape=out,
        compiler_params=params(48),
        cost_estimate=pl.CostEstimate(
            flops=4 * images * tokens * tokens * width // 3,
            bytes_accessed=3 * by_head.size,
            transcendentals=images * tokens * tokens * width // 3 // head_size,
        ),
        name="attention",
    )(by_head, by_head, by_head)


def attention_grad(by_head, grad, head_size):
    grid, specs, one, out = attention_specs(by_head)
    images, tokens, width = by_head.shape
    return pl.pallas_call(
        functools.partial(attention_grad_kernel, head_size),
        grid=grid,
        in_specs=specs + [one],
        out_specs=[one] * 3,
        out_shape=[out] * 3,
        compiler_params=params(48),
        cost_estimate=pl.CostEstimate(
            flops=10 * images * tokens * tokens * width // 3,
            bytes_accessed=5 * by_head.size,
            transcendentals=images * tokens * tokens * width // 3 // head_size,
        ),
        name="attention_grad",
    )(by_head, by_head, by_head, grad)


def exchange(values, axis, bit):
    size = lax.axis_size(axis)
    return lax.ppermute(values, axis, [(i, i ^ bit) for i in range(size)])


def bits_of(axis, lowest=1):
    size, bits = lax.axis_size(axis), []
    bit = lowest
    while bit < size:
        bits.append(bit)
        bit *= 2
    return bits


def gather_half(part, bits):
    held = part[None]
    for bit in bits:
        other = exchange(held, "dp", bit)
        held = jnp.concatenate([held, other], axis=0)
    return held.reshape((2,) * len(bits) + part.shape)


def gather_peers(part):
    bits = bits_of("dp", 2)
    count = len(bits)
    half = part.shape[1] // 2
    first = gather_half(part[:, :half], bits)
    second = gather_half(part[:, half:], bits[::-1])
    second = second.transpose(tuple(range(count))[::-1] + (count, count + 1))
    return jnp.concatenate([first, second], axis=-1).reshape(-1, part.shape[1])


def scatter_half(parts, bits):
    for bit in bits:
        other = exchange(parts[1].astype(jnp.bfloat16), "dp", bit)
        parts = parts[0].astype(jnp.float32) + other.astype(jnp.float32)
    return parts


def scatter_peers(total):
    bits = bits_of("dp", 2)
    count = len(bits)
    half = total.shape[1] // 2
    parts = total.reshape((2,) * count + (-1, total.shape[1]))
    first = scatter_half(parts[..., :half], bits[::-1])
    turned = parts[..., half:].transpose(tuple(range(count))[::-1] + (count, count + 1))
    second = scatter_half(turned, bits)
    return jnp.concatenate([first, second], axis=-1)


def scatter_blocks(values, axis, dim):
    size = lax.axis_size(axis)
    me = lax.axis_index(axis)
    bit, lead = 1, values.shape[:dim]
    shape = values.shape[dim + 1 :]
    while bit < size:
        blocks = values.shape[dim] // 2
        split = values.reshape(lead + (blocks, 2) + shape)
        mine = (me // bit) % 2
        keep = lax.dynamic_index_in_dim(split, mine, dim + 1, keepdims=False)
        send = lax.dynamic_index_in_dim(split, 1 - mine, dim + 1, keepdims=False)
        other = exchange(send.astype(jnp.bfloat16), axis, bit)
        values = keep + other.astype(jnp.float32)
        bit *= 2
    return values.reshape(lead + shape)


def body(
    vit_tokens,
    hires_map,
    norm1_gain,
    norm1_shift,
    qkv_weight,
    attn_weight,
    norm2_gain,
    norm2_shift,
    vit_fc1,
    vit_fc2,
    conv_kernel,
    conv_gain,
    conv_shift,
    conv_fc1,
    conv_fc2,
    layer_scale,
    adapter_weight,
    adapter_bias,
    adapter_kernel,
    adapter_gate,
    proj_fc1,
    proj_bias1,
    proj_fc2,
    proj_bias2,
    projected_cot,
    hires_cot,
):
    half_of = lax.rem(lax.axis_index("tile"), 2)
    width, channels = attn_weight.shape[1], conv_fc2.shape[1]

    def column_sets(matrix, count):
        sets = matrix.shape[1] // count
        return [matrix[:, i * count : (i + 1) * count] for i in range(sets)]

    def half_mlp(up_matrix, down_matrix):
        inner, outer = down_matrix.shape
        devices = lax.axis_size("dp")
        up_split = up_matrix.reshape(-1, devices, 2, inner // 2)
        up_half = lax.dynamic_index_in_dim(up_split, half_of, 2, keepdims=False)
        up_half = up_half.reshape(up_matrix.shape[0], -1)
        down_half = lax.dynamic_slice_in_dim(down_matrix, half_of * (inner // 2), inner // 2)
        return column_sets(up_half, outer) + [down_half]

    first_rows = jnp.concatenate(column_sets(qkv_weight, width) + [attn_weight])
    first_all = lax.all_gather(first_rows, "dp", axis=0, tiled=False)
    conv_all = lax.all_gather(
        jnp.concatenate(half_mlp(conv_fc1, conv_fc2)), "dp", axis=0, tiled=False
    )
    vit_rows_of = jnp.concatenate(half_mlp(vit_fc1, vit_fc2) + [adapter_weight])
    vit_all = lax.all_gather(vit_rows_of, "dp", axis=0, tiled=False)
    shard = attn_weight.shape[0]
    qkv_full = jnp.concatenate(
        [first_all[:, i * shard : (i + 1) * shard].reshape(-1, width) for i in range(3)], axis=1
    )
    attn_full = first_all[:, 3 * shard :].reshape(-1, width)
    adapter_full = vit_all[:, -adapter_weight.shape[0] :].reshape(-1, width)
    conv_half, vit_half = conv_fc2.shape[0] // 2, vit_fc2.shape[0] // 2
    conv_block, vit_block = max(384, conv_half), max(512, vit_half)
    dp_size, tile_size = lax.axis_size("dp"), lax.axis_size("tile")
    dp_index = lax.axis_index("dp")
    hidden = proj_fc2.shape[0]
    up_cols = lax.all_to_all(
        proj_fc1.reshape(-1, dp_size, hidden), "dp", split_axis=1, concat_axis=0, tiled=False
    ).reshape(-1, hidden)
    proj_up = jnp.concatenate([up_cols, exchange(up_cols, "dp", 1)], axis=1)
    proj_down = jnp.concatenate([proj_fc2, exchange(proj_fc2, "dp", 1)], axis=0)
    own_start, other_start = dp_index * hidden, (dp_index ^ 1) * hidden
    bias1_part = jnp.concatenate(
        [
            lax.dynamic_slice_in_dim(proj_bias1, own_start, hidden),
            lax.dynamic_slice_in_dim(proj_bias1, other_start, hidden),
        ]
    )
    out_grad = projected_cot.reshape(-1, projected_cot.shape[2])
    out_grads = gather_peers(out_grad)
    images = vit_tokens.shape[0]
    tok_rows = vit_tokens.shape[1]
    model_width = vit_tokens.shape[2]
    head_size = model_width // HEADS
    vit_rows = tok_rows // GV
    hires_rows = hires_map.shape[1]
    hires_cols = hires_map.shape[2]
    tokens_float = vit_tokens.astype(jnp.float32)
    normed_a, norm_a_back = jax.vjp(
        lambda values: layer_norm(values, norm1_gain, norm1_shift, EPS_VIT), tokens_float
    )
    qkv_all = product(normed_a.astype(jnp.bfloat16).reshape(-1, model_width), qkv_full).astype(
        jnp.bfloat16
    )
    qkv_all = qkv_all.reshape(images, tok_rows, 3 * model_width)
    heads_here = HEADS // tile_size
    seq_tokens = tok_rows * tile_size

    def to_heads(values, kinds):
        split = values.reshape(images, tok_rows, kinds, tile_size, heads_here * head_size)
        moved = lax.all_to_all(split, "tile", split_axis=3, concat_axis=1, tiled=False)
        return moved.reshape(images, seq_tokens, -1)

    def from_heads(values, kinds):
        split = values.reshape(images, tile_size, tok_rows, kinds, heads_here * head_size)
        moved = lax.all_to_all(split, "tile", split_axis=1, concat_axis=3, tiled=False)
        return moved.reshape(images, tok_rows, kinds * model_width)

    by_head = to_heads(qkv_all, 3)
    attended = from_heads(attention(by_head, head_size), 1).reshape(-1, model_width)
    hidden_a = tokens_float + product(attended, attn_full).reshape(images, tok_rows, model_width)
    normed_b, norm_b_back = jax.vjp(
        lambda values: layer_norm(values, norm2_gain, norm2_shift, EPS_VIT), hidden_a
    )
    vit_own, vit_other, up_a = mlp_forward(
        with_partner(normed_b.astype(jnp.bfloat16).reshape(-1, model_width)),
        vit_all,
        vit_half,
        vit_block,
    )
    vit_out = hidden_a + (vit_own + exchange(vit_other, "tile", 1).astype(jnp.float32)).reshape(
        images, tok_rows, model_width
    )
    hires_float = hires_map.astype(jnp.float32)
    hires_framed = padded(hires_map, (("tile", 1),), 3)
    conv_in, normed_c = conv_norm(hires_framed, conv_kernel, conv_gain, conv_shift, 3)
    _, norm_c_back = jax.vjp(
        lambda values: layer_norm(values, conv_gain, conv_shift, EPS_CONV), conv_in
    )
    conv_own, conv_other, up_c = mlp_forward(
        with_partner(normed_c.reshape(-1, channels)), conv_all, conv_half, conv_block
    )
    refined = hires_float + layer_scale * (
        conv_own + exchange(conv_other, "tile", 1).astype(jnp.float32)
    ).reshape(hires_map.shape)
    hires_out = refined.astype(jnp.bfloat16)
    pool = jnp.kron(pool_matrix(vit_rows, hires_rows), pool_matrix(GV, hires_cols))
    pool = pool.astype(jnp.bfloat16)
    pooled_low = jnp.einsum(
        "pr,irc->ipc",
        pool,
        hires_out.reshape(images, -1, channels),
        preferred_element_type=jnp.float32,
    )
    pooled_low = pooled_low.astype(jnp.bfloat16).reshape(-1, channels)
    adapted = (product(pooled_low, adapter_full) + adapter_bias).astype(jnp.bfloat16)
    adapted = adapted.reshape(images, vit_rows, GV, model_width)
    adapted_framed = padded(adapted, (("tile", 1),), 1)
    mixed_map = depthwise_rows(adapted_framed, adapter_kernel, 1).reshape(
        images, tok_rows, model_width
    )
    gate_value = jnp.tanh(adapter_gate)
    merged = vit_out + gate_value * mixed_map
    merged_low = merged.astype(jnp.bfloat16).reshape(-1, model_width)
    merged_all = gather_peers(merged_low)
    pre_act = product(merged_all, proj_up) + bias1_part
    act_p, gelu_p_back = jax.vjp(jax.nn.gelu, pre_act)
    act_p_low = act_p.astype(jnp.bfloat16)
    projected = (
        (scatter_peers(product(act_p_low, proj_down).astype(jnp.bfloat16)) + proj_bias2)
        .astype(jnp.bfloat16)
        .reshape(images, tok_rows, -1)
    )
    bias2_grad = jnp.sum(out_grad.astype(jnp.float32), axis=0)
    pre_grad = gelu_p_back(times_transposed(out_grads, proj_down))[0].astype(jnp.bfloat16)
    merged_grad = scatter_peers(
        times_transposed(pre_grad, proj_up).astype(jnp.bfloat16)
    ).reshape(images, tok_rows, model_width)
    fc2_part = row_contract(act_p_low, out_grads)
    fc2_part = fc2_part[:hidden] + exchange(
        fc2_part[hidden:].astype(jnp.bfloat16), "dp", 1
    ).astype(jnp.float32)
    fc2_grad = scatter_blocks(
        fc2_part.reshape(tile_size, -1, fc2_part.shape[1]), "tile", 0
    )
    fc1_part = row_contract(merged_all, pre_grad)
    fc1_part = fc1_part[:, :hidden] + exchange(
        fc1_part[:, hidden:].astype(jnp.bfloat16), "dp", 1
    ).astype(jnp.float32)
    fc1_part = scatter_blocks(
        fc1_part.reshape(dp_size, tile_size, -1, hidden), "tile", 1
    )
    fc1_grad = lax.all_to_all(
        fc1_part.astype(jnp.bfloat16), "dp", split_axis=0, concat_axis=1, tiled=False
    )
    fc1_grad = fc1_grad.reshape(fc1_grad.shape[0], -1).astype(jnp.float32)
    bias1_sum = jnp.sum(pre_grad.astype(jnp.float32), axis=0)
    bias1_grad = jnp.zeros_like(proj_bias1)
    bias1_grad = lax.dynamic_update_slice_in_dim(bias1_grad, bias1_sum[:hidden], own_start, 0)
    bias1_grad = lax.dynamic_update_slice_in_dim(bias1_grad, bias1_sum[hidden:], other_start, 0)
    gate_grad = jnp.sum(merged_grad * mixed_map, axis=(0, 1)) * (1.0 - gate_value * gate_value)
    mixed_grad = (gate_value * merged_grad).reshape(images, vit_rows, GV, model_width)
    mixed_framed = padded(mixed_grad.astype(jnp.bfloat16), (("tile", 1),), 1).astype(
        mixed_grad.dtype
    )
    kernel_grad = kernel_terms(adapted_framed, mixed_grad, 1)
    adapted_grad = (
        depthwise_rows(mixed_framed, adapter_kernel[::-1], 1)
        .astype(jnp.bfloat16)
        .reshape(-1, model_width)
    )
    bias_a_grad = jnp.sum(adapted_grad.astype(jnp.float32), axis=0)
    adapter_part = row_contract(pooled_low, adapted_grad)
    adapter_part = adapter_part.reshape(dp_size, tile_size, -1, model_width)
    adapter_grad = scatter_blocks(scatter_blocks(adapter_part, "dp", 0), "tile", 0)
    pooled_grad = times_transposed(adapted_grad, adapter_full).astype(jnp.bfloat16)
    unpooled = jnp.einsum(
        "pr,ipc->irc",
        pool,
        pooled_grad.reshape(images, -1, channels),
        preferred_element_type=jnp.float32,
    ).reshape(hires_map.shape)
    refined_grad = hires_cot.astype(jnp.float32) + unpooled
    branch_grad = (layer_scale * refined_grad).astype(jnp.bfloat16).reshape(-1, channels)
    conv_own, conv_other = mlp_backward(
        with_partner(branch_grad), up_c, conv_all, conv_half, conv_block
    )
    normed_c_grad = conv_own + exchange(conv_other, "tile", 1).astype(jnp.float32)
    conv_in_grad = norm_c_back(normed_c_grad.reshape(hires_map.shape))[0]
    conv_framed = padded(conv_in_grad.astype(jnp.bfloat16), (("tile", 1),), 3)
    hires_grad = conv_add(conv_framed, conv_kernel[::-1], refined_grad, 3)
    down_grad = merged_grad.astype(jnp.bfloat16).reshape(-1, model_width)
    vit_own, vit_other = mlp_backward(
        with_partner(down_grad), up_a, vit_all, vit_half, vit_block
    )
    normed_b_grad = vit_own + exchange(vit_other, "tile", 1).astype(jnp.float32)
    hidden_grad = merged_grad + norm_b_back(normed_b_grad.reshape(merged_grad.shape))[0]
    attn_grad = hidden_grad.astype(jnp.bfloat16).reshape(-1, model_width)
    attended_grad = to_heads(
        times_transposed(attn_grad, attn_full)
        .astype(jnp.bfloat16)
        .reshape(images, tok_rows, model_width),
        1,
    )
    qkv_grad = jnp.stack(attention_grad(by_head, attended_grad, head_size), axis=2)
    qkv_grad = from_heads(qkv_grad, 3).reshape(-1, 3 * model_width)
    tokens_grad = (
        hidden_grad
        + norm_a_back(times_transposed(qkv_grad, qkv_full).reshape(images, tok_rows, model_width))[
            0
        ]
    )
    bias2_grad, bias1_grad, bias_a_grad, kernel_grad, gate_grad = lax.psum(
        (bias2_grad, bias1_grad, bias_a_grad, kernel_grad, gate_grad), ("dp", "tile")
    )
    return (
        projected,
        hires_out,
        tokens_grad,
        hires_grad,
        adapter_grad,
        bias_a_grad,
        kernel_grad,
        gate_grad,
        fc1_grad,
        bias1_grad,
        fc2_grad,
        bias2_grad,
    )


def solution(mesh):
    in_specs = (
        P("dp", "tile", None),
        P("dp", "tile", None, None),
        P(),
        P(),
        P("dp", None),
        P("dp", None),
        P(),
        P(),
        P("dp", None),
        P("dp", None),
        P(),
        P(),
        P(),
        P("dp", None),
        P("dp", None),
        P(),
        P("dp", None),
        P(),
        P(),
        P(),
        P("dp", None),
        P(),
        P("dp", None),
        P(),
        P("dp", "tile", None),
        P("dp", "tile", None, None),
    )
    out_specs = (
        P("dp", "tile", None),
        P("dp", "tile", None, None),
        P("dp", "tile", None),
        P("dp", "tile", None, None),
        P(("dp", "tile"), None),
        P(),
        P(),
        P(),
        P(("dp", "tile"), None),
        P(),
        P(("dp", "tile"), None),
        P(),
    )
    return jax.shard_map(body, mesh=mesh, in_specs=in_specs, out_specs=out_specs, check_vma=False)
```

time: 2980 us -> 922 us (0.31)
  waiting for transfers between devices: 2470 us -> 323 us
  matrix products: 273 us -> 81.3 us
  Pallas kernels: 0 us -> 154 us
  starting transfers between devices: 26.9 us -> 100 us
  local copies, waits for them, and re-layouts: 78.1 us -> 135 us
    reduce_scatter x4 -> x0, waiting for transfers between devices: 1900 us -> none  [the longest x3 1900 us: summed_rows(): lax.psum_scatter(term_fn(jnp.int32(0), lax.axis_size(('dp', 'tile')) * (t...]
    all_gather x10 -> x3, waiting for transfers between devices: 529 us -> 32.7 us  [the longest x1 32.7 us: body(): first_all = lax.all_gather(first_rows, 'dp', axis=0, tiled=False)]
    ppermute x0 -> x37, waiting for transfers between devices: none -> 213 us  [exchange(): return lax.ppermute(values, axis, [(i, i ^ bit) for i in range(size)])]
    pallas_call x0 -> x8, Pallas kernels: none -> 154 us  [the longest x2 53.7 us: mlp_backward(): pl.pallas_call(mlp_backward_kernel, grid=(hidden // block,), in_specs=[pl...]
    dot_general x9 -> x5, matrix products: 93.9 us -> 27.4 us  [product(): return jnp.dot(left, right, preferred_element_type=jnp.float32)]
    ppermute x4, waiting for transfers between devices: 9.93 us -> 74.9 us  [padded(): after = lax.ppermute(leading, axis, down)]
    ppermute x0 -> x37, starting transfers between devices: none -> 51.7 us  [exchange(): return lax.ppermute(values, axis, [(i, i ^ bit) for i in range(size)])]
    dot_general x9 -> x2, matrix products: 52.7 us -> 1.01 us  [the longest x1 0.62 us: body(): jnp.einsum('pr,ipc->irc', pool, pooled_grad.reshape(images, -1, channels)...]
  transfers between devices with their start and end apart: 23 -> 55, of which waited for: 16 -> 17; matrix products, arithmetic and copies ran while one was open for 12% -> 24% of each run, Pallas kernels for 0% -> 17%
where the time goes in v1:
time: 922 us; the launch traced here: 913 us
  waiting for transfers between devices  323 us (35%)
  Pallas kernels  154 us (17%)
  local copies, waits for them, and re-layouts  135 us (15%)
  other arithmetic  103 us (11%)
  starting transfers between devices  100 us (11%)
  matrix products  81.3 us (9%)
  between operations  16.2 us (2%)
    ppermute x37, waiting for transfers between devices, exchange(): return lax.ppermute(values, axis, [(i, i ^ bit) for i in range(size)])  213 us
    ppermute x4, waiting for transfers between devices, padded(): after = lax.ppermute(leading, axis, down)  74.9 us
    pallas_call x2, Pallas kernels, mlp_backward(): pl.pallas_call(mlp_backward_kernel, grid=(hidden // block,), in_specs=[pl...  53.7 us
    ppermute x37, starting transfers between devices, exchange(): return lax.ppermute(values, axis, [(i, i ^ bit) for i in range(size)])  51.7 us
    pallas_call x2, Pallas kernels, mlp_forward(): pl.pallas_call(mlp_forward_kernel, grid=(hidden // block,), in_specs=[pl....  51.4 us
    unnamed x218, local copies, waits for them, and re-layouts  36.7 us
    all_gather x1, waiting for transfers between devices, body(): first_all = lax.all_gather(first_rows, 'dp', axis=0, tiled=False)  32.7 us
    dot_general x5, matrix products, times_transposed(): lax.dot_general(left, right, (((1,), (1,)), ((), ())), preferred_element_...  28.5 us
  transfers between devices with their start and end apart: 55, of which 17 were waited for; matrix products, arithmetic and copies ran while one was open for 24% of the time, Pallas kernels for 17%

profile of v1, /device:TPU:0, one launch (start us, length us, event | category | flops | bytes accessed | tf_op | source)
XLA Modules:
  0.0 912.7 jit_solution(14079886888118134628)
XLA Ops:
  15.3 8.8 dynamic-slice_reduce_fusion
  35.1 32.7 %all-gather.7.cloned.1.call-done = bf16[4096,1024]{1,0:T(8,128)(2,1)} async-done(((bf16[512,1024]{1,0:T(8,128)(2,1)}), bf16[4096,1024]{1,0:T(8,128)(2,1)}) %all-gather.7.cloned.1.call-update) | async-done | bytes 8388624 | tf_op jit(solution)/shard_map/all_gather | solution.py:544
  67.8 4.8 fusion.98
  89.8 5.4 collective-permute-start.2
  104.0 27.3 %collective-permute-done.3 = bf16[2,3,32,1536]{3,2,1,0:T(8,128)(2,1)} collective-permute-done((bf16[2,3,32,1536]{3,2,1,0:T(8,128)(2,1)}, bf16[2,3,32,1536]{3,2,1,0:T(8,128)(2,1)}, u32[]{:S(2)}, u32[]{:S(2)}) %collective-permute-start.3) | collective-permute-done | bytes 589856 | tf_op jit(solution)/shard_map/ppermute | solution.py:26
  132.9 14.9 %conv_norm.1 = (f32[2,8,32,1536]{3,2,1,0:T(8,128)S(1)}, bf16[2,8,32,1536]{3,2,1,0:T(8,128)(2,1)}) custom-call(bf16[2,14,32,1536]{3,2,1,0:T(8,128)(2,1)S(1)} %pad_maximum_fusion.10.map_ref, f32[49,1536]{1,0:T(8,128)S(1)} %copy-done.7, f32[1,1536]{1,0:T(1,128)S(1)} %broadcast_in_dim.30.gain_ref, f32[1,1536]{1,0:T(1,128)S(1)} %broadcast_in_dim.31.shift_ref), custom_call_target="tpu_custom_call" | custom-call | flops 77070336 | bytes 7864320 | tf_op jit(solution)/shard_map/conv_norm/pallas_call | solution.py:312
  147.8 11.0 %collective-permute-start.4 = (bf16[512,1536]{1,0:T(8,128)(2,1)}, bf16[512,1536]{1,0:T(8,128)(2,1)}, u32[]{:S(2)}, u32[]{:S(2)}) collective-permute-start(bf16[512,1536]{1,0:T(8,128)(2,1)} %bitcast.15), channel_id=1, source_target_pairs={{0,1},{1,0},{2,3},{3,2},{4,5},{5,4},{6,7},{7,6},{8,9},{9,8},{10,11... | collective-permute-start | bytes 4718600 | tf_op jit(solution)/shard_map/ppermute | solution.py:434
  173.2 5.6 reshape_squeeze.10.q_ref.k_ref.v_ref
  180.6 8.3 attention.1
  219.0 39.7 %mlp_forward.3 = (f32[512,1536]{1,0:T(8,128)}, bf16[512,1536]{1,0:T(8,128)(2,1)}, bf16[1024,3072]{1,0:T(8,128)(2,1)}) custom-call(bf16[1024,1536]{1,0:T(8,128)(2,1)} %pad_maximum_fusion.8.x_ref, bf16[8,768,1536]{2,1,0:T(8,128)(2,1)} %bitcast.384, bf16[8,768,1536]{2,1,0:T(8,128)(2,1)} %bitcast.385), custom_call_target="tpu_custom_call" | custom-call | flops 19327352832 | bytes 37748736 | tf_op jit(solution)/shard_map/mlp_forward/pallas_call | solution.py:188
  264.5 39.7 %collective-permute-done.21 = bf16[2,288,2048]{2,1,0:T(8,128)(2,1)} collective-permute-done((bf16[2,288,2048]{2,1,0:T(8,128)(2,1)}, bf16[2,288,2048]{2,1,0:T(8,128)(2,1)}, u32[]{:S(2)}, u32[]{:S(2)}) %collective-permute-start.21) | collective-permute-done | bytes 2359328 | tf_op jit(solution)/shard_map/ppermute | solution.py:434
  312.7 11.7 %mlp_forward.2 = (f32[288,1024]{1,0:T(8,128)}, bf16[288,1024]{1,0:T(8,128)(2,1)}, bf16[576,2048]{1,0:T(8,128)(2,1)}) custom-call(bf16[576,1024]{1,0:T(8,128)(2,1)} %pad_maximum_fusion.25.x_ref, bf16[8,704,1024]{2,1,0:T(8,128)(2,1)} %bitcast.270, bf16[8,704,1024]{2,1,0:T(8,128)(2,1)} %bitcast.271), custom_call_target="tpu_custom_call" | custom-call | flops 4831838208 | bytes 15466496 | tf_op jit(solution)/shard_map/mlp_forward/pallas_call | solution.py:188
  333.0 7.8 collective-permute-done.1
  349.0 9.6 %collective-permute-done.19 = bf16[2,288,2048]{2,1,0:T(8,128)(2,1)} collective-permute-done((bf16[2,288,2048]{2,1,0:T(8,128)(2,1)}, bf16[2,288,2048]{2,1,0:T(8,128)(2,1)}, u32[]{:S(2)}, u32[]{:S(2)}) %collective-permute-start.19) | collective-permute-done | bytes 2359328 | tf_op jit(solution)/shard_map/ppermute | solution.py:434
  388.3 14.9 %convolution_convert_fusion = bf16[1152,4096]{1,0:T(8,128)(2,1)S(1)} fusion(bf16[1024,4096]{1,0:T(8,128)(2,1)} %constant_dynamic-update-slice_fusion, f32[1152,1024]{1,0:T(8,128)S(1)} %convolution_add_fusion), kind=kOutput, calls=%fused_computation | convolution fusion | flops 9679011840 | bytes 22544384 | tf_op jit(solution)/shard_map/dot_general | solution.py:39
  410.0 19.5 %convert_reduce_fusion.1 = (f32[1024]{0:T(1024)S(1)}, bf16[1152,1024]{1,0:T(8,128)(2,1)}) fusion(f32[1152,1024]{1,0:T(8,128)} %copy-done.95, bf16[1024,4096]{1,0:T(8,128)(2,1)} %constant_dynamic-update-slice_fusion, bf16[1152,2048]{1,0:T(8,128)(2,1)} %bitcast.316, bf16[1152,2048]{1,0:T(8,128)(2,1)} %bitcast.314), kind=kOutput, calls=%fused_computation.27 | convolution fusion | flops 9708502016 | bytes 24907776 | tf_op jit(solution)/shard_map/dot_general | solution.py:43
  429.5 4.9 convolution_convert_fusion.2
  436.6 19.7 %fusion.2 = f32[1024,4096]{1,0:T(8,128)} fusion(bf16[1152,2048]{1,0:T(8,128)(2,1)} %bitcast.317, bf16[1152,2048]{1,0:T(8,128)(2,1)} %bitcast.315, f32[1152,1024]{1,0:T(8,128)} %copy-done.95), kind=kOutput, calls=%fused_computation.9 | convolution fusion | flops 9693167616 | bytes 30932992 | tf_op jit(solution)/shard_map/dot_general | solution.py:49
  465.4 56.1 %collective-permute-done.24 = bf16[2,288,512]{2,1,0:T(8,128)(2,1)S(1)} collective-permute-done((bf16[2,288,512]{2,1,0:T(8,128)(2,1)S(1)}, bf16[2,288,512]{2,1,0:T(8,128)(2,1)S(1)}, u32[]{:S(2)}, u32[]{:S(2)}) %collective-permute-start.24) | collective-permute-done | bytes 589856 | tf_op jit(solution)/shard_map/ppermute | solution.py:434
  528.0 6.0 slice.512
  563.3 12.1 %mlp_backward.2 = (f32[288,1024]{1,0:T(8,128)}, bf16[288,1024]{1,0:T(8,128)(2,1)}) custom-call(bf16[576,1024]{1,0:T(8,128)(2,1)} %pad_maximum_fusion.29.y_ref, bf16[576,2048]{1,0:T(8,128)(2,1)} %get-tuple-element.32.up_ref, bf16[8,704,1024]{2,1,0:T(8,128)(2,1)} %bitcast.272, bf16[8,704,1024]{2,1,0:T(8,128)(2,1)} %bitcast.273), custom_call_target="tpu_custom_call" | custom-call | flops 4831838208 | bytes 15466496 | tf_op jit(solution)/shard_map/mlp_backward/pallas_call | solution.py:214
  584.7 10.0 %collective-permute-done.41 = bf16[8,1,32,512]{3,2,0,1:T(8,128)(2,1)} collective-permute-done((bf16[8,1,32,512]{3,2,0,1:T(8,128)(2,1)S(1)}, bf16[8,1,32,512]{3,2,0,1:T(8,128)(2,1)}, u32[]{:S(2)}, u32[]{:S(2)}) %collective-permute-start.41) | collective-permute-done | bytes 262176 | tf_op jit(solution)/shard_map/ppermute | solution.py:434
  615.1 5.5 convert_add_fusion
  643.4 41.6 %mlp_backward.3 = (f32[512,1536]{1,0:T(8,128)}, bf16[512,1536]{1,0:T(8,128)(2,1)}) custom-call(bf16[1024,1536]{1,0:T(8,128)(2,1)} %pad_maximum_fusion.9.y_ref, bf16[1024,3072]{1,0:T(8,128)(2,1)} %get-tuple-element.38.up_ref, bf16[8,768,1536]{2,1,0:T(8,128)(2,1)} %bitcast.386, bf16[8,768,1536]{2,1,0:T(8,128)(2,1)} %bitcast.387), custom_call_target="tpu_custom_call" | custom-call | flops 19327352832 | bytes 37748736 | tf_op jit(solution)/shard_map/mlp_backward/pallas_call | solution.py:214
  685.1 13.8 %attention_grad.1 = (bf16[2,576,256]{2,1,0:T(8,128)(2,1)S(1)}, bf16[2,576,256]{2,1,0:T(8,128)(2,1)S(1)}, bf16[2,576,256]{2,1,0:T(8,128)(2,1)S(1)}) custom-call(bf16[2,576,768]{2,1,0:T(8,128)(2,1)S(1)} %copy-done.5, bf16[2,576,768]{2,1,0:T(8,128)(2,1)S(1)} %copy-done.5, bf16[2,576,768]{2,1,0:T(8,128)(2,1)S(1)} %copy-done.5, bf16[2,576,256]{2,1,0:T(8,128)(2,1)S(1)} %bitcast.268), custom_call_target="tpu_custom_call" | custom-call | flops 1698693120 | bytes 4423680 | tf_op jit(solution)/shard_map/attention_grad/pallas_call | solution.py:416
  700.4 4.9 all-to-all-start.4
  719.4 32.9 %collective-permute-done.37 = bf16[2,48,1024]{2,1,0:T(8,128)(2,1)S(1)} collective-permute-done((bf16[2,48,1024]{2,1,0:T(8,128)(2,1)S(1)}, bf16[2,48,1024]{2,1,0:T(8,128)(2,1)S(1)}, u32[]{:S(2)}, u32[]{:S(2)}) %collective-permute-start.37) | collective-permute-done | bytes 196640 | tf_op jit(solution)/shard_map/ppermute | solution.py:434
  759.1 9.5 %slice_add_fusion = f32[512,4096]{1,0:T(8,128)} fusion(f32[1024,4096]{1,0:T(8,128)} %fusion.2, bf16[512,4096]{1,0:T(8,128)(2,1)} %collective-permute-done.42), kind=kLoop, calls=%fused_computation.3 | loop fusion | flops 4194304 | bytes 20971520 | tf_op jit(solution)/shard_map/add | solution.py:664
  776.2 4.9 collective-permute-start.32
  783.6 47.6 %collective-permute-done.33 = bf16[2,3,32,1536]{3,2,1,0:T(8,128)(2,1)S(1)} collective-permute-done((bf16[2,3,32,1536]{3,2,1,0:T(8,128)(2,1)S(1)}, bf16[2,3,32,1536]{3,2,1,0:T(8,128)(2,1)S(1)}, u32[]{:S(2)}, u32[]{:S(2)}) %collective-permute-start.33) | collective-permute-done | bytes 589856 | tf_op jit(solution)/shard_map/ppermute | solution.py:26
  831.5 12.0 %conv_add.1 = f32[2,8,32,1536]{3,2,1,0:T(8,128)} custom-call(bf16[2,14,32,1536]{3,2,1,0:T(8,128)(2,1)S(1)} %pad_maximum_fusion.11.map_ref, f32[49,1536]{1,0:T(8,128)S(1)} %rev.4.taps_ref, f32[2,8,32,1536]{3,2,1,0:T(8,128)S(1)} %copy-done.6), custom_call_target="tpu_custom_call" | custom-call | flops 77070336 | bytes 7864320 | tf_op jit(solution)/shard_map/conv_add/pallas_call | solution.py:330
  857.6 39.8 %collective-permute-done.44 = bf16[1,128,4096]{2,1,0:T(8,128)(2,1)S(1)} collective-permute-done((bf16[1,128,4096]{2,1,0:T(8,128)(2,1)S(1)}, bf16[1,128,4096]{2,1,0:T(8,128)(2,1)S(1)}, u32[]{:S(2)}, u32[]{:S(2)}) %collective-permute-start.44) | collective-permute-done | bytes 1048608 | tf_op jit(solution)/shard_map/ppermute | solution.py:434
  (483 shorter events, 313.6 us)
Async XLA Ops:
  7.2 60.6 %all-gather.7.cloned.1.call-start = ((), (), s32[]{:S(2)}) async-start(), calls=%async_computation.6 | async-start | bytes 9437184 | tf_op jit(solution)/shard_map/all_gather | solution.py:544
  10.6 208.4 %all-gather.11.cloned.1.call-start = ((), (), s32[]{:S(2)}) async-start(), calls=%async_computation.8 | async-start | bytes 21233664 | tf_op jit(solution)/shard_map/all_gather | solution.py:545
  26.1 284.4 %all-gather.9.cloned.1.call-start = ((), (), s32[]{:S(2)}) async-start(), calls=%async_computation.7 | async-start | bytes 12976128 | tf_op jit(solution)/shard_map/all_gather | solution.py:549
  32.6 336.8 %collective-permute-start.13 = (bf16[512,4096]{1,0:T(8,128)(2,1)}, bf16[512,4096]{1,0:T(8,128)(2,1)}, u32[]{:S(2)}, u32[]{:S(2)}) collective-permute-start(bf16[512,4096]{1,0:T(8,128)(2,1)} %param.48), channel_id=1, source_target_pairs={{0,4},{4,0},{8,12},{12,8},{16,20},{20,16},{24,28},{28,24},{1,5},{5... | collective-permute-start | bytes 12582920 | tf_op jit(solution)/shard_map/ppermute | solution.py:434
  82.6 76.2 %all-to-all-start = ((bf16[2,1,144,3,4,256]{5,2,3,1,0,4:T(8,128)(2,1)}), bf16[2,1,144,3,4,256]{5,2,3,1,0,4:T(8,128)(2,1)}, u32[]{:S(2)}, u32[]{:S(2)}) async-start(bf16[2,1,144,3,4,256]{5,2,3,1,0,4:T(8,128)(2,1)} %copy.101), calls=%async_computation | async-start | bytes 3538944 | tf_op jit(solution)/shard_map/all_to_all | solution.py:595
  88.5 42.8 %collective-permute-start.3 = (bf16[2,3,32,1536]{3,2,1,0:T(8,128)(2,1)}, bf16[2,3,32,1536]{3,2,1,0:T(8,128)(2,1)}, u32[]{:S(2)}, u32[]{:S(2)}) collective-permute-start(bf16[2,3,32,1536]{3,2,1,0:T(8,128)(2,1)} %get-tuple-element.74), channel_id=1, source_target_pairs={{1,0},{2,1},{3,2},{5,4},{6,5},{7,6},{9,8},{10,9},{11,10},{13,12},{... | collective-permute-start | bytes 1769480 | tf_op jit(solution)/shard_map/ppermute | solution.py:26
  89.8 41.5 %collective-permute-start.2 = (bf16[2,3,32,1536]{3,2,1,0:T(8,128)(2,1)}, bf16[2,3,32,1536]{3,2,1,0:T(8,128)(2,1)}, u32[]{:S(2)}, u32[]{:S(2)}) collective-permute-start(bf16[2,3,32,1536]{3,2,1,0:T(8,128)(2,1)} %get-tuple-element.73), channel_id=1, source_target_pairs={{0,1},{1,2},{2,3},{4,5},{5,6},{6,7},{8,9},{9,10},{10,11},{12,13},{... | collective-permute-start | bytes 1769480 | tf_op jit(solution)/shard_map/ppermute | solution.py:25
  96.8 107.7 %collective-permute-start.20 = (bf16[1,288,2048]{2,1,0:T(8,128)(2,1)}, bf16[1,288,2048]{2,1,0:T(8,128)(2,1)}, u32[]{:S(2)}, u32[]{:S(2)}) collective-permute-start(bf16[1,288,2048]{2,1,0:T(8,128)(2,1)} %get-tuple-element.70), channel_id=1, source_target_pairs={{0,16},{4,20},{8,24},{12,28},{16,0},{20,4},{24,8},{28,12},{1,17},{... | collective-permute-start | bytes 3538952 | tf_op jit(solution)/shard_map/ppermute | solution.py:434
  97.9 162.8 %collective-permute-start.18 = (bf16[1,288,2048]{2,1,0:T(8,128)(2,1)}, bf16[1,288,2048]{2,1,0:T(8,128)(2,1)}, u32[]{:S(2)}, u32[]{:S(2)}) collective-permute-start(bf16[1,288,2048]{2,1,0:T(8,128)(2,1)} %get-tuple-element.69), channel_id=1, source_target_pairs={{0,8},{4,12},{8,0},{12,4},{16,24},{20,28},{24,16},{28,20},{1,9},{5... | collective-permute-start | bytes 3538952 | tf_op jit(solution)/shard_map/ppermute | solution.py:434
  147.8 61.2 %collective-permute-start.4 = (bf16[512,1536]{1,0:T(8,128)(2,1)}, bf16[512,1536]{1,0:T(8,128)(2,1)}, u32[]{:S(2)}, u32[]{:S(2)}) collective-permute-start(bf16[512,1536]{1,0:T(8,128)(2,1)} %bitcast.15), channel_id=1, source_target_pairs={{0,1},{1,0},{2,3},{3,2},{4,5},{5,4},{6,7},{7,6},{8,9},{9,8},{10,11... | collective-permute-start | bytes 4718600 | tf_op jit(solution)/shard_map/ppermute | solution.py:434
  194.6 704.4 %all-reduce.5.cloned.1.call-start = ((), (), s32[]{:S(2)}) async-start(), calls=%async_computation.9 | async-start | bytes 212992 | tf_op jit(solution)/shard_map/psum | solution.py:737
  204.4 178.7 %collective-permute-start.12 = (bf16[1024,512]{1,0:T(8,128)(2,1)}, bf16[1024,512]{1,0:T(8,128)(2,1)}, u32[]{:S(2)}, u32[]{:S(2)}) collective-permute-start(bf16[1024,512]{1,0:T(8,128)(2,1)} %bitcast.44), channel_id=1, source_target_pairs={{0,4},{4,0},{8,12},{12,8},{16,20},{20,16},{24,28},{28,24},{1,5},{5... | collective-permute-start | bytes 3145736 | tf_op jit(solution)/shard_map/ppermute | solution.py:434
  207.6 96.5 %collective-permute-start.21 = (bf16[2,288,2048]{2,1,0:T(8,128)(2,1)}, bf16[2,288,2048]{2,1,0:T(8,128)(2,1)}, u32[]{:S(2)}, u32[]{:S(2)}) collective-permute-start(bf16[2,288,2048]{2,1,0:T(8,128)(2,1)} %pad_maximum_fusion.17), channel_id=1, source_target_pairs={{0,8},{4,12},{8,0},{12,4},{16,24},{20,28},{24,16},{28,20},{1,9},{5... | collective-permute-start | bytes 7077896 | tf_op jit(solution)/shard_map/ppermute | solution.py:434
  258.7 67.6 %collective-permute-start.5 = (bf16[512,1536]{1,0:T(8,128)(2,1)}, bf16[512,1536]{1,0:T(8,128)(2,1)}, u32[]{:S(2)}, u32[]{:S(2)}) collective-permute-start(bf16[512,1536]{1,0:T(8,128)(2,1)} %get-tuple-element.31), channel_id=1, source_target_pairs={{0,1},{1,0},{2,3},{3,2},{4,5},{5,4},{6,7},{7,6},{8,9},{9,8},{10,11... | collective-permute-start | bytes 4718600 | tf_op jit(solution)/shard_map/ppermute | solution.py:434
  260.7 48.7 %collective-permute-start = (bf16[288,1024]{1,0:T(8,128)(2,1)S(1)}, bf16[288,1024]{1,0:T(8,128)(2,1)S(1)}, u32[]{:S(2)}, u32[]{:S(2)}) collective-permute-start(bf16[288,1024]{1,0:T(8,128)(2,1)S(1)} %bitcast.335), channel_id=1, source_target_pairs={{0,1},{1,0},{2,3},{3,2},{4,5},{5,4},{6,7},{7,6},{8,9},{9,8},{10,11... | collective-permute-start | bytes 1769480 | tf_op jit(solution)/shard_map/ppermute | solution.py:434
  304.2 54.4 %collective-permute-start.19 = (bf16[2,288,2048]{2,1,0:T(8,128)(2,1)}, bf16[2,288,2048]{2,1,0:T(8,128)(2,1)}, u32[]{:S(2)}, u32[]{:S(2)}) collective-permute-start(bf16[2,288,2048]{2,1,0:T(8,128)(2,1)} %pad_maximum_fusion.16), channel_id=1, source_target_pairs={{0,16},{4,20},{8,24},{12,28},{16,0},{20,4},{24,8},{28,12},{1,17},{... | collective-permute-start | bytes 7077896 | tf_op jit(solution)/shard_map/ppermute | solution.py:434
  458.1 157.0 %collective-permute-start.16 = (bf16[2,288,2048]{2,1,0:T(8,128)(2,1)}, bf16[2,288,2048]{2,1,0:T(8,128)(2,1)}, u32[]{:S(2)}, u32[]{:S(2)}) collective-permute-start(bf16[2,288,2048]{2,1,0:T(8,128)(2,1)} %slice_bitcast_fusion.2), channel_id=1, source_target_pairs={{0,8},{4,12},{8,0},{12,4},{16,24},{20,28},{24,16},{28,20},{1,9},{5... | collective-permute-start | bytes 7077896 | tf_op jit(solution)/shard_map/ppermute | solution.py:434
  458.9 166.5 %collective-permute-start.14 = (bf16[2,288,2048]{2,1,0:T(8,128)(2,1)}, bf16[2,288,2048]{2,1,0:T(8,128)(2,1)}, u32[]{:S(2)}, u32[]{:S(2)}) collective-permute-start(bf16[2,288,2048]{2,1,0:T(8,128)(2,1)} %slice_bitcast_fusion.5), channel_id=1, source_target_pairs={{0,16},{4,20},{8,24},{12,28},{16,0},{20,4},{24,8},{28,12},{1,17},{... | collective-permute-start | bytes 7077896 | tf_op jit(solution)/shard_map/ppermute | solution.py:434
  459.2 62.3 %collective-permute-start.24 = (bf16[2,288,512]{2,1,0:T(8,128)(2,1)S(1)}, bf16[2,288,512]{2,1,0:T(8,128)(2,1)S(1)}, u32[]{:S(2)}, u32[]{:S(2)}) collective-permute-start(bf16[2,288,512]{2,1,0:T(8,128)(2,1)S(1)} %slice_bitcast_fusion.10), channel_id=1, source_target_pairs={{0,8},{4,12},{8,0},{12,4},{16,24},{20,28},{24,16},{28,20},{1,9},{5... | collective-permute-start | bytes 1769480 | tf_op jit(solution)/shard_map/ppermute | solution.py:434
  460.3 62.3 %collective-permute-start.22 = (bf16[2,288,512]{2,1,0:T(8,128)(2,1)S(1)}, bf16[2,288,512]{2,1,0:T(8,128)(2,1)S(1)}, u32[]{:S(2)}, u32[]{:S(2)}) collective-permute-start(bf16[2,288,512]{2,1,0:T(8,128)(2,1)S(1)} %copy-done.65), channel_id=1, source_target_pairs={{0,16},{4,20},{8,24},{12,28},{16,0},{20,4},{24,8},{28,12},{1,17},{... | collective-permute-start | bytes 1769480 | tf_op jit(solution)/shard_map/ppermute | solution.py:434
  545.9 213.2 %collective-permute-start.42 = (bf16[512,4096]{1,0:T(8,128)(2,1)}, bf16[512,4096]{1,0:T(8,128)(2,1)}, u32[]{:S(2)}, u32[]{:S(2)}) collective-permute-start(bf16[512,4096]{1,0:T(8,128)(2,1)} %slice.512), channel_id=1, source_target_pairs={{0,4},{4,0},{8,12},{12,8},{16,20},{20,16},{24,28},{28,24},{1,5},{5... | collective-permute-start | bytes 12582920 | tf_op jit(solution)/shard_map/ppermute | solution.py:434
  594.7 45.5 %collective-permute-start.30 = (bf16[512,1536]{1,0:T(8,128)(2,1)}, bf16[512,1536]{1,0:T(8,128)(2,1)}, u32[]{:S(2)}, u32[]{:S(2)}) collective-permute-start(bf16[512,1536]{1,0:T(8,128)(2,1)} %bitcast.312), channel_id=1, source_target_pairs={{0,1},{1,0},{2,3},{3,2},{4,5},{5,4},{6,7},{7,6},{8,9},{9,8},{10,11... | collective-permute-start | bytes 4718600 | tf_op jit(solution)/shard_map/ppermute | solution.py:434
  610.5 74.5 %all-to-all-start.3 = ((bf16[2,1,144,1,4,256]{5,2,0,3,1,4:T(8,128)(2,1)}), bf16[2,1,144,1,4,256]{5,2,0,3,1,4:T(8,128)(2,1)S(1)}, u32[]{:S(2)}, u32[]{:S(2)}) async-start(bf16[2,1,144,1,4,256]{5,2,0,3,1,4:T(8,128)(2,1)} %copy.114), calls=%async_computation.3 | async-start | bytes 1179648 | tf_op jit(solution)/shard_map/all_to_all | solution.py:595
  623.6 85.1 %collective-permute-start.17 = (bf16[288,2048]{1,0:T(8,128)(2,1)}, bf16[288,2048]{1,0:T(8,128)(2,1)}, u32[]{:S(2)}, u32[]{:S(2)}) collective-permute-start(bf16[288,2048]{1,0:T(8,128)(2,1)} %fusion.51), channel_id=1, source_target_pairs={{0,16},{4,20},{8,24},{12,28},{16,0},{20,4},{24,8},{28,12},{1,17},{... | collective-permute-start | bytes 3538952 | tf_op jit(solution)/shard_map/ppermute | solution.py:434
  630.1 87.7 %collective-permute-start.15 = (bf16[288,2048]{1,0:T(8,128)(2,1)}, bf16[288,2048]{1,0:T(8,128)(2,1)}, u32[]{:S(2)}, u32[]{:S(2)}) collective-permute-start(bf16[288,2048]{1,0:T(8,128)(2,1)} %fusion.50), channel_id=1, source_target_pairs={{0,8},{4,12},{8,0},{12,4},{16,24},{20,28},{24,16},{28,20},{1,9},{5... | collective-permute-start | bytes 3538952 | tf_op jit(solution)/shard_map/ppermute | solution.py:434
  636.2 69.2 %collective-permute-start.35 = (bf16[2,4,48,1024]{3,2,1,0:T(8,128)(2,1)}, bf16[2,4,48,1024]{3,2,1,0:T(8,128)(2,1)}, u32[]{:S(2)}, u32[]{:S(2)}) collective-permute-start(bf16[2,4,48,1024]{3,2,1,0:T(8,128)(2,1)} %fusion.72), channel_id=1, source_target_pairs={{0,8},{4,12},{8,0},{12,4},{16,24},{20,28},{24,16},{28,20},{1,9},{5... | collective-permute-start | bytes 2359304 | tf_op jit(solution)/shard_map/ppermute | solution.py:434
  685.0 70.1 %collective-permute-start.31 = (bf16[512,1536]{1,0:T(8,128)(2,1)}, bf16[512,1536]{1,0:T(8,128)(2,1)}, u32[]{:S(2)}, u32[]{:S(2)}) collective-permute-start(bf16[512,1536]{1,0:T(8,128)(2,1)} %get-tuple-element.40), channel_id=1, source_target_pairs={{0,1},{1,0},{2,3},{3,2},{4,5},{5,4},{6,7},{7,6},{8,9},{9,8},{10,11... | collective-permute-start | bytes 4718600 | tf_op jit(solution)/shard_map/ppermute | solution.py:434
  700.4 143.1 %all-to-all-start.4 = ((bf16[2,4,144,3,1,256]{5,2,0,4,3,1:T(8,128)(2,1)}), bf16[2,4,144,3,1,256]{5,2,0,4,3,1:T(8,128)(2,1)}, u32[]{:S(2)}, u32[]{:S(2)}) async-start(bf16[2,4,144,3,1,256]{5,2,0,4,3,1:T(8,128)(2,1)} %copy.127), calls=%async_computation.4 | async-start | bytes 3538944 | tf_op jit(solution)/shard_map/all_to_all | solution.py:600
  772.4 75.2 %collective-permute-start.43 = (bf16[2,128,4096]{2,1,0:T(8,128)(2,1)}, bf16[2,128,4096]{2,1,0:T(8,128)(2,1)}, u32[]{:S(2)}, u32[]{:S(2)}) collective-permute-start(bf16[2,128,4096]{2,1,0:T(8,128)(2,1)} %fusion.14), channel_id=1, source_target_pairs={{0,1},{1,0},{2,3},{3,2},{4,5},{5,4},{6,7},{7,6},{8,9},{9,8},{10,11... | collective-permute-start | bytes 6291464 | tf_op jit(solution)/shard_map/ppermute | solution.py:434
  774.9 56.3 %collective-permute-start.33 = (bf16[2,3,32,1536]{3,2,1,0:T(8,128)(2,1)S(1)}, bf16[2,3,32,1536]{3,2,1,0:T(8,128)(2,1)S(1)}, u32[]{:S(2)}, u32[]{:S(2)}) collective-permute-start(bf16[2,3,32,1536]{3,2,1,0:T(8,128)(2,1)S(1)} %get-tuple-element.72), channel_id=1, source_target_pairs={{1,0},{2,1},{3,2},{5,4},{6,5},{7,6},{9,8},{10,9},{11,10},{13,12},{... | collective-permute-start | bytes 1769480 | tf_op jit(solution)/shard_map/ppermute | solution.py:26
  776.2 55.0 %collective-permute-start.32 = (bf16[2,3,32,1536]{3,2,1,0:T(8,128)(2,1)S(1)}, bf16[2,3,32,1536]{3,2,1,0:T(8,128)(2,1)S(1)}, u32[]{:S(2)}, u32[]{:S(2)}) collective-permute-start(bf16[2,3,32,1536]{3,2,1,0:T(8,128)(2,1)S(1)} %get-tuple-element.71), channel_id=1, source_target_pairs={{0,1},{1,2},{2,3},{4,5},{5,6},{6,7},{8,9},{9,10},{10,11},{12,13},{... | collective-permute-start | bytes 1769480 | tf_op jit(solution)/shard_map/ppermute | solution.py:25
  851.5 45.9 %collective-permute-start.44 = (bf16[1,128,4096]{2,1,0:T(8,128)(2,1)S(1)}, bf16[1,128,4096]{2,1,0:T(8,128)(2,1)S(1)}, u32[]{:S(2)}, u32[]{:S(2)}) collective-permute-start(bf16[1,128,4096]{2,1,0:T(8,128)(2,1)S(1)} %dynamic-slice_convert_fusion.1), channel_id=1, source_target_pairs={{0,2},{1,3},{2,0},{3,1},{4,6},{5,7},{6,4},{7,5},{8,10},{9,11},{10,... | collective-permute-start | bytes 3145736 | tf_op jit(solution)/shard_map/ppermute | solution.py:434
  (127 other events, 1356.2 us)
Sparse Core Ops, SparseCore 0:
  10.7 57.0 all-gather.6
  70.3 127.5 all-gather.10
  199.8 109.5 all-gather.8
  584.8 122.9 all-reduce.4
